TPU v7x, 512 devices: a whole 4x8x8 slice. The times are simulated.
512 devices in a mesh: occ: 8 (over z_hi, core), ao: 64 (over y, x, z_lo).
Axes of the slice: x: 4, y: 8, z: 8 (z_hi: 4, z_lo: 2; z = z_hi * 2 + z_lo), core: 2. Of those that a mesh axis runs over, the one named last changes fastest.
Arguments:
- integrals: bfloat16 [98304, 4096], P(('occ', 'ao')), may hold values from -0.5 to 0.5
- tile_owner: int32 [98304, 1], P(('occ', 'ao')), may hold values from 0 to 63; in each aligned block of 192 rows (0 to 191, 192 to 383, ...) at most 4 rows name the same one
- tile_blocks: int32 [98304, 3], P(('occ', 'ao')), may hold values from 0 to 255
- nu_offset: int32 [98304, 1], P(('occ', 'ao')), may hold values from 0 to 3
- pair_list: int32 [32, 2], replicated, may hold values from 0 to 255
- occ_coef: bfloat16 [2048, 256], P('ao'), may hold values from -6 to 6
- vir_coef: bfloat16 [2048, 1792], P('ao'), may hold values from -0.125 to 0.125
Outputs:
- exchange_ints: float32 [32, 1792, 1792], P('occ', 'ao')
Inputs may be any that keep to these rules, and one draw needn't show every extreme that they name: `tile_owner`: among the rows of one device no value appears more than 4 times.
All inputs are finite; a program needn't handle non-finite values.
Results may differ from a plain program's by a relative error of at most 0.0048.
Values may be sent and summed in bfloat16 or wider, within the bound.
A program may use at most 64 MiB of HBM per device.

v0:
```python
import jax
import jax.numpy as jnp
from jax import lax
from jax.sharding import PartitionSpec as P

SHELL_FUNCTIONS = 8
CAP = 4
NBLK = 256


def shell_rows(shell_ids, columns, shell_total):
    pair_count = columns.shape[1]
    flat_cols = columns.reshape(shell_total, SHELL_FUNCTIONS * pair_count)
    shell_table = jnp.arange(shell_total, dtype=jnp.int32)[None, :]
    picker = (shell_ids[:, None] == shell_table).astype(jnp.bfloat16)
    chosen = jnp.dot(picker, flat_cols, preferred_element_type=jnp.float32)
    return chosen.reshape(shell_ids.shape[0], SHELL_FUNCTIONS, pair_count)


def shards(integrals, tile_owner, tile_blocks, nu_offset, pair_list, occ_coef, vir_coef):
    ao_count = lax.axis_size("ao")
    occ_count = lax.axis_size("occ")
    occ_full, vir_full = (
        lax.all_gather(occ_coef, "ao", axis=0, tiled=True),
        lax.all_gather(vir_coef, "ao", axis=0, tiled=True),
    )
    orbital_count = occ_full.shape[1]
    pair_count = pair_list.shape[0]
    orbital_ids = jnp.arange(orbital_count, dtype=jnp.int32)[:, None]
    pick_left = (orbital_ids == pair_list[None, :, 0]).astype(jnp.bfloat16)
    pick_right = (orbital_ids == pair_list[None, :, 1]).astype(jnp.bfloat16)
    left_cols = jnp.dot(occ_full, pick_left, preferred_element_type=jnp.float32).astype(
        jnp.bfloat16
    )
    right_cols = jnp.dot(occ_full, pick_right, preferred_element_type=jnp.float32).astype(
        jnp.bfloat16
    )
    tile_count = integrals.shape[0]
    tile_mats = integrals.reshape(
        tile_count, SHELL_FUNCTIONS * SHELL_FUNCTIONS, SHELL_FUNCTIONS * SHELL_FUNCTIONS
    )
    left_row_block = shell_rows(tile_blocks[:, 0], left_cols, NBLK)
    right_row_block = shell_rows(tile_blocks[:, 1], right_cols, NBLK)
    density_matrix = jnp.einsum("ndy,noy->nydo", left_row_block, right_row_block).reshape(
        tile_count, pair_count, SHELL_FUNCTIONS * SHELL_FUNCTIONS
    )
    product = jnp.einsum(
        "tpk,tkn->tpn",
        density_matrix,
        tile_mats.astype(jnp.float32),
        precision=lax.Precision.HIGHEST,
    )
    partial_rows = product.astype(jnp.bfloat16)
    owners = tile_owner[:, 0]
    order_ids = jnp.arange(tile_count, dtype=jnp.int32)
    earlier_same = (owners[:, None] == owners[None, :]) & (order_ids[None, :] < order_ids[:, None])
    slot_index = jnp.sum(earlier_same.astype(jnp.int32), axis=1)
    per_owner = NBLK // ao_count
    pairs_local = pair_count // occ_count
    destination = owners * CAP + slot_index
    slot_table = jnp.arange(ao_count * CAP, dtype=jnp.int32)[:, None]
    dispatch = slot_table == destination[None, :]
    flat_rows = partial_rows.reshape(tile_count, pair_count * SHELL_FUNCTIONS * SHELL_FUNCTIONS)
    outgoing = jnp.dot(
        dispatch.astype(jnp.bfloat16), flat_rows, preferred_element_type=jnp.float32
    ).astype(jnp.bfloat16)
    outgoing = outgoing.reshape(
        ao_count, CAP, occ_count, pairs_local * SHELL_FUNCTIONS * SHELL_FUNCTIONS
    )
    block_ids = nu_offset[:, 0] * NBLK + tile_blocks[:, 2]
    slot_ids = jnp.sum(jnp.where(dispatch, block_ids[None, :], 0), axis=1)
    outgoing_ids = jnp.broadcast_to(
        slot_ids.reshape(ao_count, CAP, 1, 1), (ao_count, CAP, occ_count, 1)
    )
    received, received_ids = (
        lax.all_to_all(
            lax.all_to_all(outgoing, "ao", split_axis=0, concat_axis=1, tiled=True),
            "occ",
            split_axis=2,
            concat_axis=1,
            tiled=True,
        ),
        lax.all_to_all(
            lax.all_to_all(outgoing_ids, "ao", split_axis=0, concat_axis=1, tiled=True),
            "occ",
            split_axis=2,
            concat_axis=1,
            tiled=True,
        ),
    )
    received_ids = received_ids.reshape(-1)
    received = received.reshape(
        received_ids.shape[0], pairs_local * SHELL_FUNCTIONS * SHELL_FUNCTIONS
    )
    target_table = jnp.arange(per_owner * NBLK, dtype=jnp.int32)[:, None]
    collector = (target_table == received_ids[None, :]).astype(jnp.bfloat16)
    sums = jnp.dot(collector, received, preferred_element_type=jnp.float32)
    half_field = sums.reshape(
        per_owner, NBLK, pairs_local, SHELL_FUNCTIONS, SHELL_FUNCTIONS
    ).transpose(2, 0, 3, 1, 4)
    half_field = half_field.reshape(
        pairs_local, per_owner * SHELL_FUNCTIONS, NBLK * SHELL_FUNCTIONS
    ).astype(jnp.bfloat16)
    virtual_rows = jnp.einsum(
        "pns,sb->pbn", half_field, vir_full, preferred_element_type=jnp.float32
    ).astype(jnp.bfloat16)
    return jnp.einsum(
        "pbn,na->pba",
        lax.all_to_all(virtual_rows, "ao", split_axis=1, concat_axis=2, tiled=True),
        vir_full,
        preferred_element_type=jnp.float32,
    )


def solution(mesh):
    placed = (
        P(("occ", "ao"), None),
        P(("occ", "ao"), None),
        P(("occ", "ao"), None),
        P(("occ", "ao"), None),
        P(),
        P("ao", None),
        P("ao", None),
    )
    return jax.shard_map(
        shards, mesh=mesh, in_specs=placed, out_specs=P("occ", "ao", None), check_vma=False
    )
```

profile of v0, /device:TPU:56, one launch (start us, length us, event | category | flops | bytes accessed | tf_op | source)
XLA Modules:
  0.0 686.4 jit_solution(421760321684674047)
XLA Ops:
  6.5 0.0 all-gather.3.cloned.1.call-start
  6.5 0.7 all-gather.3.cloned.1.call-update
  7.3 0.0 all-gather.5.cloned.1.call-start
  7.3 0.7 all-gather.5.cloned.1.call-update
  8.0 3.8 copy.71
  11.8 0.0 copy-start
  11.8 0.0 copy-start.3
  11.8 0.0 copy-start.1
  11.9 0.0 copy-start.2
  11.9 4.3 copy.73
  16.1 0.0 copy-done
  16.1 0.2 convert_reduce_fusion
  16.3 0.0 copy-done.3
  16.4 0.0 copy-done.1
  16.4 0.0 copy-done.2
  16.4 285.7 %all-gather.3.cloned.1.call-done = bf16[2048,256]{1,0:T(8,128)(2,1)} async-done(((bf16[32,256]{1,0:T(8,128)(2,1)}), bf16[2048,256]{1,0:T(8,128)(2,1)}) %all-gather.3.cloned.1.call-update) | async-done | bytes 1048592 | tf_op jit(solution)/shard_map/all_gather | solution.py:24
  302.1 1.6 fusion.15
  303.8 1.0 copy.65
  304.8 1.4 reshape.84
  306.2 0.1 copy.66
  306.3 0.3 convolution_bitcast_fusion.1
  306.6 0.2 copy.67
  306.8 1.6 fusion.16
  308.4 1.0 copy.68
  309.4 2.1 reshape.85
  311.5 1.0 copy.69
  312.5 0.3 convolution_bitcast_fusion
  312.8 0.2 copy.70
  313.0 1.6 multiply_bitcast_fusion
  314.6 4.0 copy.72
  318.6 5.0 convolution_convert_fusion.3
  323.6 2.4 copy.74
  326.0 0.6 convolution_convert_fusion
  326.6 1.3 copy.87
  327.9 18.4 %all-to-all-start.2 = ((bf16[64,4,8,256]{3,2,1,0:T(8,128)(2,1)}), bf16[64,4,8,256]{3,2,1,0:T(8,128)(2,1)S(1)}, u32[]{:S(2)}, u32[]{:S(2)}) async-start(bf16[64,4,8,256]{3,2,1,0:T(8,128)(2,1)} %bitcast.47), calls=%async_computation.2 | async-start | bytes 2097152 | tf_op jit(solution)/shard_map/all_to_all | solution.py:77
  346.2 0.1 select_reduce_fusion
  346.4 0.1 broadcast_in_dim.18
  346.5 18.4 %all-to-all-done.2 = bf16[64,4,8,256]{3,2,1,0:T(8,128)(2,1)S(1)} async-done(((bf16[64,4,8,256]{3,2,1,0:T(8,128)(2,1)}), bf16[64,4,8,256]{3,2,1,0:T(8,128)(2,1)S(1)}, u32[]{:S(2)}, u32[]{:S(2)}) %all-to-all-start.2) | async-done | bytes 1048608 | tf_op jit(solution)/shard_map/all_to_all | solution.py:77
  364.9 0.8 broadcast_in_dim.19
  365.7 9.8 %all-to-all-start = ((s32[64,4,8,1]{2,1,3,0:T(4,128)}), s32[64,4,8,1]{2,1,3,0:T(4,128)S(1)}, u32[]{:S(2)}, u32[]{:S(2)}) async-start(s32[64,4,8,1]{2,1,3,0:T(4,128)} %broadcast_in_dim.19), calls=%async_computation | async-start | bytes 262144 | tf_op jit(solution)/shard_map/all_to_all | solution.py:84
  375.4 1.2 copy.84
  376.6 8.1 %all-to-all-done = s32[64,4,8,1]{2,1,3,0:T(4,128)S(1)} async-done(((s32[64,4,8,1]{2,1,3,0:T(4,128)}), s32[64,4,8,1]{2,1,3,0:T(4,128)S(1)}, u32[]{:S(2)}, u32[]{:S(2)}) %all-to-all-start) | async-done | bytes 8224 | tf_op jit(solution)/shard_map/all_to_all | solution.py:84
  384.7 6.7 all-to-all-start.3
  391.5 0.7 copy.64
  392.1 37.8 %all-to-all-done.3 = bf16[1,256,8,256]{3,1,0,2:T(8,128)(2,1)S(1)} async-done(((bf16[1,256,8,256]{3,1,0,2:T(8,128)(2,1)}), bf16[1,256,8,256]{3,1,0,2:T(8,128)(2,1)S(1)}, u32[]{:S(2)}, u32[]{:S(2)}) %all-to-all-start.3) | async-done | bytes 1048608 | tf_op jit(solution)/shard_map/all_to_all | solution.py:76
  430.0 6.9 %all-to-all-start.1 = ((s32[1,256,8,1]{1,3,0,2:T(1,128)}), s32[1,256,8,1]{1,3,0,2:T(1,128)S(1)}, u32[]{:S(2)}, u32[]{:S(2)}) async-start(s32[1,256,8,1]{1,3,0,2:T(1,128)} %copy.64), calls=%async_computation.1 | async-start | bytes 16384 | tf_op jit(solution)/shard_map/all_to_all | solution.py:83
  436.8 0.6 copy.76
  437.5 7.1 %all-to-all-done.1 = s32[1,256,8,1]{1,3,0,2:T(1,128)S(1)} async-done(((s32[1,256,8,1]{1,3,0,2:T(1,128)}), s32[1,256,8,1]{1,3,0,2:T(1,128)S(1)}, u32[]{:S(2)}, u32[]{:S(2)}) %all-to-all-start.1) | async-done | bytes 8224 | tf_op jit(solution)/shard_map/all_to_all | solution.py:83
  444.6 1.6 fusion.20
  446.2 5.8 copy.77
  451.9 12.8 %convert_element_type.52 = bf16[4,32,2048]{2,1,0:T(8,128)(2,1)S(1)} reshape(bf16[4,4,8,256,8]{4,3,2,1,0:T(8,128)(2,1)} %copy.77) | data formatting | bytes 1048576 | tf_op jit(solution)/shard_map/convert_element_type | solution.py:103
  464.8 163.6 %all-gather.5.cloned.1.call-done = bf16[2048,1792]{1,0:T(8,128)(2,1)} async-done(((bf16[32,1792]{1,0:T(8,128)(2,1)}), bf16[2048,1792]{1,0:T(8,128)(2,1)}) %all-gather.5.cloned.1.call-update) | async-done | bytes 7340048 | tf_op jit(solution)/shard_map/all_gather | solution.py:25
  628.4 4.2 fusion.12
  632.6 1.9 copy.78
  634.5 1.3 reshape.96
  635.9 31.8 %all_to_all.72 = bf16[64,2,1792]{2,1,0:T(2,128)(2,1)S(1)} all-to-all(bf16[64,2,1792]{2,1,0:T(2,128)(2,1)S(1)} %reshape.96), channel_id=1, replica_groups=mesh['occ'=8,'ao'=64] {'ao'}, dimensions={0} | all-to-all | bytes 917504 | tf_op jit(solution)/shard_map/all_to_all | solution.py:109
  667.7 1.0 reshape.97
  668.7 1.8 copy.91
  670.5 3.2 all_to_all.66
  673.7 4.4 fusion.3
  678.1 1.4 copy.82
  (4 shorter events, 0.0 us)
Async XLA Ops:
  6.5 295.6 %all-gather.3.cloned.1.call-start = ((), (), s32[]{:S(2)}) async-start(), calls=%async_computation.5 | async-start | bytes 1064960 | tf_op jit(solution)/shard_map/all_gather | solution.py:24
  7.3 621.2 %all-gather.5.cloned.1.call-start = ((), (), s32[]{:S(2)}) async-start(), calls=%async_computation.6 | async-start | bytes 7454720 | tf_op jit(solution)/shard_map/all_gather | solution.py:25
  11.8 4.3 copy-start
  11.8 4.5 copy-start.3
  11.8 4.5 copy-start.1
  11.9 4.5 copy-start.2
  327.9 37.0 %all-to-all-start.2 = ((bf16[64,4,8,256]{3,2,1,0:T(8,128)(2,1)}), bf16[64,4,8,256]{3,2,1,0:T(8,128)(2,1)S(1)}, u32[]{:S(2)}, u32[]{:S(2)}) async-start(bf16[64,4,8,256]{3,2,1,0:T(8,128)(2,1)} %bitcast.47), calls=%async_computation.2 | async-start | bytes 2097152 | tf_op jit(solution)/shard_map/all_to_all | solution.py:77
  365.7 19.1 %all-to-all-start = ((s32[64,4,8,1]{2,1,3,0:T(4,128)}), s32[64,4,8,1]{2,1,3,0:T(4,128)S(1)}, u32[]{:S(2)}, u32[]{:S(2)}) async-start(s32[64,4,8,1]{2,1,3,0:T(4,128)} %broadcast_in_dim.19), calls=%async_computation | async-start | bytes 262144 | tf_op jit(solution)/shard_map/all_to_all | solution.py:84
  384.7 45.2 %all-to-all-start.3 = ((bf16[1,256,8,256]{3,1,0,2:T(8,128)(2,1)}), bf16[1,256,8,256]{3,1,0,2:T(8,128)(2,1)S(1)}, u32[]{:S(2)}, u32[]{:S(2)}) async-start(bf16[1,256,8,256]{3,1,0,2:T(8,128)(2,1)} %copy.84), calls=%async_computation.3 | async-start | bytes 2097152 | tf_op jit(solution)/shard_map/all_to_all | solution.py:76
  430.0 14.6 %all-to-all-start.1 = ((s32[1,256,8,1]{1,3,0,2:T(1,128)}), s32[1,256,8,1]{1,3,0,2:T(1,128)S(1)}, u32[]{:S(2)}, u32[]{:S(2)}) async-start(s32[1,256,8,1]{1,3,0,2:T(1,128)} %copy.64), calls=%async_computation.1 | async-start | bytes 16384 | tf_op jit(solution)/shard_map/all_to_all | solution.py:83
Sparse Core Ops, SparseCore 0:
  9.4 292.6 all-gather.2
  304.2 324.1 all-gather.4
where the time goes:
time: 688 us; the launch traced here: 686 us
  waiting for transfers between devices  522 us (76%)
  local copies, waits for them, and re-layouts  55.4 us (8%)
  starting transfers between devices  41.8 us (6%)
  blocking collectives  31.8 us (5%)
  matrix products  19.5 us (3%)
  between operations  13.6 us (2%)
    all_gather x1, waiting for transfers between devices, shards(): lax.all_gather(occ_coef, 'ao', axis=0, tiled=True)  286 us
    all_gather x1, waiting for transfers between devices, shards(): lax.all_gather(vir_coef, 'ao', axis=0, tiled=True)  164 us
    all_to_all x1, waiting for transfers between devices, shards(): lax.all_to_all(lax.all_to_all(outgoing, 'ao', split_axis=0, concat_axis=1...  37.8 us
    all_to_all x1, blocking collectives, shards(): lax.all_to_all(virtual_rows, 'ao', split_axis=1, concat_axis=2, tiled=True)  31.8 us
    convert_element_type x2, local copies, waits for them, and re-layouts, shards(): half_field = half_field.reshape(pairs_local, per_owner * SHELL_FUNCTIONS,...  18.6 us
    all_to_all x1, waiting for transfers between devices, shards(): lax.all_to_all(outgoing, 'ao', split_axis=0, concat_axis=1, tiled=True)  18.4 us
    all_to_all x1, starting transfers between devices, shards(): lax.all_to_all(outgoing, 'ao', split_axis=0, concat_axis=1, tiled=True)  18.4 us
  transfers between devices with their start and end apart: 6, of which 6 were waited for; matrix products, arithmetic and copies ran while one was open for 8% of the time, Pallas kernels for 0%

commit v1 on v0

--- a/solution.py
+++ b/solution.py
@@ -1,11 +1,130 @@
 import jax
 import jax.numpy as jnp
 from jax import lax
+from jax.experimental import pallas as pl
+from jax.experimental.pallas import tpu as pltpu
 from jax.sharding import PartitionSpec as P
 
 SHELL_FUNCTIONS = 8
 CAP = 4
 NBLK = 256
+NY, NX, NZ = 8, 4, 2
+N_AO = 64
+MESH = pl.DeviceIdType.MESH
+
+
+def remote(src, dst, send, recv, occ, ao):
+    return pltpu.make_async_remote_copy(
+        src_ref=src, dst_ref=dst, send_sem=send, recv_sem=recv,
+        device_id=(occ, ao), device_id_type=MESH,
+    )
+
+
+def gather_kernel(sel_ref, vir_ref, sel_out, vir_out, loc, sel_s, sel_r, y_s, y_r, z_s, z_r, x_s, x_r, c_s, c_r):
+    occ = lax.axis_index("occ")
+    ao = lax.axis_index("ao")
+    half = lax.rem(occ, 2)
+    sibling = occ + 1 - 2 * half
+    zl = lax.rem(ao, NZ)
+    x = lax.rem(ao // NZ, NX)
+    y = ao // (NZ * NX)
+
+    def ao_of(yy, xx, zz):
+        return (yy * NX + xx) * NZ + zz
+
+    barrier = pltpu.get_barrier_semaphore()
+
+    def greet(k, carry):
+        pl.semaphore_signal(barrier, inc=1, device_id=(occ, lax.rem(ao + k, N_AO)), device_id_type=MESH)
+        return carry
+
+    lax.fori_loop(1, N_AO, greet, 0)
+    pl.semaphore_signal(barrier, inc=1, device_id=(sibling, ao), device_id_type=MESH)
+    pl.semaphore_wait(barrier, N_AO)
+
+    own = [
+        pltpu.make_async_copy(sel_ref, sel_out.at[ao], loc.at[0]),
+        pltpu.make_async_copy(vir_ref.at[half], vir_out.at[y, x, zl, half], loc.at[1]),
+    ]
+    for copy in own:
+        copy.start()
+
+    def y_copy(k):
+        yy = lax.rem(y + k, NY)
+        return remote(vir_ref.at[half], vir_out.at[y, x, zl, half], y_s.at[k], y_r.at[k], occ, ao_of(yy, x, zl))
+
+    def sel_copy(k):
+        return remote(sel_ref, sel_out.at[ao], sel_s.at[k], sel_r.at[k], occ, lax.rem(ao + k, N_AO))
+
+    def start_sel(k, carry):
+        sel_copy(k).start()
+        return carry
+
+    lax.fori_loop(1, N_AO, start_sel, 0)
+    for k in range(1, NY):
+        y_copy(k).start()
+    for copy in own:
+        copy.wait()
+    for k in range(1, NY):
+        y_copy(k).wait()
+    z_copy = remote(vir_out.at[:, x, zl, half], vir_out.at[:, x, zl, half], z_s, z_r, occ, ao_of(y, x, 1 - zl))
+    z_copy.start()
+    z_copy.wait()
+    right, left = lax.rem(x + 1, NX), lax.rem(x + NX - 1, NX)
+    far = lax.rem(x + 2, NX)
+
+    def x_copy(n, block, lo, hi, to):
+        ref = vir_out.at[lo:hi, block, :, half]
+        return remote(ref, ref, x_s.at[n], x_r.at[n], occ, ao_of(y, to, zl))
+
+    def c_copy(n, block):
+        ref = vir_out.at[:, block, :, half]
+        return remote(ref, ref, c_s.at[n], c_r.at[n], sibling, ao)
+
+    to_right = x_copy(0, x, 0, NY, right)
+    to_left = x_copy(1, x, 0, NY, left)
+    to_right.start()
+    to_left.start()
+    c_copies = [c_copy(0, x), c_copy(1, left), c_copy(2, right), c_copy(3, far)]
+    to_right.wait_recv()
+    fwd_right = x_copy(2, left, 0, NY // 2, right)
+    fwd_right.start()
+    to_left.wait_recv()
+    fwd_left = x_copy(3, right, NY // 2, NY, left)
+    fwd_left.start()
+    for copy in c_copies[:3]:
+        copy.start()
+    to_right.wait_send()
+    to_left.wait_send()
+    fwd_right.wait()
+    fwd_left.wait()
+    c_copies[3].start()
+    for copy in c_copies:
+        copy.wait()
+
+    def end_sel(k, carry):
+        sel_copy(k).wait()
+        return carry
+
+    lax.fori_loop(1, N_AO, end_sel, 0)
+
+
+def gather(sel, vir):
+    dma = pltpu.SemaphoreType.DMA
+    return pl.pallas_call(
+        gather_kernel,
+        out_shape=(
+            jax.ShapeDtypeStruct((N_AO, 16, 128), jnp.bfloat16),
+            jax.ShapeDtypeStruct((NY, NX, NZ, 2, 16, vir.shape[-1]), jnp.bfloat16),
+        ),
+        in_specs=[pl.BlockSpec(memory_space=pl.ANY)] * 2,
+        out_specs=[pl.BlockSpec(memory_space=pl.ANY)] * 2,
+        scratch_shapes=[
+            dma((2,)), dma((N_AO,)), dma((N_AO,)), dma((NY,)), dma((NY,)), dma, dma,
+            dma((4,)), dma((4,)), dma((4,)), dma((4,)),
+        ],
+        compiler_params=pltpu.CompilerParams(collective_id=0, has_side_effects=True),
+    )(sel, vir)
 
 
 def shell_rows(shell_ids, columns, shell_total):
@@ -20,21 +139,18 @@
 def shards(integrals, tile_owner, tile_blocks, nu_offset, pair_list, occ_coef, vir_coef):
     ao_count = lax.axis_size("ao")
     occ_count = lax.axis_size("occ")
-    occ_full, vir_full = (
-        lax.all_gather(occ_coef, "ao", axis=0, tiled=True),
-        lax.all_gather(vir_coef, "ao", axis=0, tiled=True),
-    )
-    orbital_count = occ_full.shape[1]
+    orbital_count = occ_coef.shape[1]
     pair_count = pair_list.shape[0]
     orbital_ids = jnp.arange(orbital_count, dtype=jnp.int32)[:, None]
-    pick_left = (orbital_ids == pair_list[None, :, 0]).astype(jnp.bfloat16)
-    pick_right = (orbital_ids == pair_list[None, :, 1]).astype(jnp.bfloat16)
-    left_cols = jnp.dot(occ_full, pick_left, preferred_element_type=jnp.float32).astype(
-        jnp.bfloat16
-    )
-    right_cols = jnp.dot(occ_full, pick_right, preferred_element_type=jnp.float32).astype(
-        jnp.bfloat16
-    )
+    both = jnp.concatenate([pair_list[:, 0], pair_list[:, 1]])
+    pick = (orbital_ids == both[None, :]).astype(jnp.bfloat16)
+    sel = jnp.dot(occ_coef, pick, preferred_element_type=jnp.float32).astype(jnp.bfloat16)
+    sel = jnp.concatenate([sel[:16], sel[16:]], axis=1)
+    cols, vir = gather(sel, vir_coef.reshape(2, 16, vir_coef.shape[1]))
+    vir_full = vir.reshape(-1, vir_coef.shape[1])
+    cols = cols.reshape(ao_count, 16, 2, 2 * pair_count).transpose(0, 2, 1, 3).reshape(-1, 2 * pair_count)
+    left_cols = cols[:, :pair_count]
+    right_cols = cols[:, pair_count:]
     tile_count = integrals.shape[0]
     tile_mats = integrals.reshape(
         tile_count, SHELL_FUNCTIONS * SHELL_FUNCTIONS, SHELL_FUNCTIONS * SHELL_FUNCTIONS

time: 688 us -> 281 us (0.41)
  waiting for transfers between devices: 522 us -> 70.8 us
  Pallas kernels: 0 us -> 76.5 us
  starting transfers between devices: 41.8 us -> 28.3 us
  between operations: 13.6 us -> 0.27 us
  blocking collectives: 31.8 us -> 22.6 us
    all_gather x2 -> x0, waiting for transfers between devices: 449 us -> none  [the longest x1 286 us: shards(): lax.all_gather(occ_coef, 'ao', axis=0, tiled=True)]
    pallas_call x0 -> x1, Pallas kernels: none -> 76.5 us  [gather(): pl.pallas_call(gather_kernel, out_shape=(jax.ShapeDtypeStruct((N_AO, 16,...]
    all_to_all x1, starting transfers between devices: 18.4 us -> 8.41 us  [shards(): lax.all_to_all(outgoing, 'ao', split_axis=0, concat_axis=1, tiled=True)]
    all_to_all x1, waiting for transfers between devices: 37.8 us -> 28 us  [shards(): lax.all_to_all(lax.all_to_all(outgoing, 'ao', split_axis=0, concat_axis=1...]
    all_to_all x1, waiting for transfers between devices: 18.4 us -> 28.1 us  [shards(): lax.all_to_all(outgoing, 'ao', split_axis=0, concat_axis=1, tiled=True)]
    all_to_all x1, blocking collectives: 31.8 us -> 22.6 us  [shards(): lax.all_to_all(virtual_rows, 'ao', split_axis=1, concat_axis=2, tiled=True)]
  transfers between devices with their start and end apart: 6 -> 4, of which waited for: 6 -> 4; matrix products, arithmetic and copies ran while one was open for 8% -> 1% of each run, Pallas kernels for 0% -> 0%
where the time goes in v1:
time: 281 us; the launch traced here: 279 us
  Pallas kernels  76.5 us (27%)
  waiting for transfers between devices  70.8 us (25%)
  local copies, waits for them, and re-layouts  58.3 us (21%)
  starting transfers between devices  28.3 us (10%)
  blocking collectives  22.6 us (8%)
  matrix products  17.1 us (6%)
  other arithmetic  5.29 us (2%)
    pallas_call x1, Pallas kernels, gather(): pl.pallas_call(gather_kernel, out_shape=(jax.ShapeDtypeStruct((N_AO, 16,...  76.5 us
    all_to_all x1, waiting for transfers between devices, shards(): lax.all_to_all(outgoing, 'ao', split_axis=0, concat_axis=1, tiled=True)  28.1 us
    all_to_all x1, waiting for transfers between devices, shards(): lax.all_to_all(lax.all_to_all(outgoing, 'ao', split_axis=0, concat_axis=1...  28 us
    all_to_all x1, blocking collectives, shards(): lax.all_to_all(virtual_rows, 'ao', split_axis=1, concat_axis=2, tiled=True)  22.6 us
    convert_element_type x2, local copies, waits for them, and re-layouts, shards(): half_field = half_field.reshape(pairs_local, per_owner * SHELL_FUNCTIONS,...  18.6 us
    all_to_all x1, starting transfers between devices, shards(): lax.all_to_all(lax.all_to_all(outgoing, 'ao', split_axis=0, concat_axis=1...  9.4 us
    all_to_all x1, starting transfers between devices, shards(): lax.all_to_all(outgoing, 'ao', split_axis=0, concat_axis=1, tiled=True)  8.41 us
    all_to_all x1, waiting for transfers between devices, shards(): lax.all_to_all(outgoing_ids, 'ao', split_axis=0, concat_axis=1, tiled=True)  7.94 us
  transfers between devices with their start and end apart: 4, of which 4 were waited for; matrix products, arithmetic and copies ran while one was open for 1% of the time, Pallas kernels for 0%

profile of v1, /device:TPU:56, one launch (start us, length us, event | category | flops | bytes accessed | tf_op | source)
XLA Modules:
  0.0 279.2 jit_solution(16687984208912159472)
XLA Ops:
  0.0 0.0 copy-start
  0.0 0.9 convert_reduce_fusion
  0.9 1.3 multiply_add_fusion.1
  2.2 0.8 slice_bitcast_fusion.1
  3.0 0.1 pad_add_fusion
  3.0 0.0 copy-done
  3.0 0.1 fusion.12
  3.2 3.8 %copy.52 = bf16[192,4096]{0,1:T(8,128)(2,1)} copy(bf16[192,4096]{1,0:T(8,128)(2,1)} %param.7) | data formatting | bytes 3145728 | tf_op args[0]
  7.0 4.2 %copy.54 = bf16[192,64,64]{2,1,0:T(8,128)(2,1)S(1)} copy(bf16[192,64,64]{0,2,1:T(8,128)(2,1)} %bitcast.93) | data formatting | bytes 3145728 | tf_op jit(solution)/shard_map/reshape | solution.py:155
  11.3 0.0 copy-start.3
  11.3 0.0 copy-start.4
  11.3 0.7 pad_maximum_fusion.sel_ref
  12.0 76.5 %shard_map.73 = (bf16[64,16,128]{2,1,0:T(8,128)(2,1)}, bf16[8,4,2,2,16,1792]{5,4,3,2,1,0:T(8,128)(2,1)}) custom-call(bf16[16,128]{1,0:T(8,128)(2,1)} %pad_maximum_fusion.sel_ref, bf16[2,16,1792]{2,1,0:T(8,128)(2,1)} %bitcast.108), custom_call_target="tpu_custom_call" | custom-call | tf_op jit(solution)/shard_map/pallas_call | solution.py:114
  88.5 2.0 reshape.97
  90.5 1.1 copy.47
  91.6 1.2 fusion.26
  92.8 1.4 reshape.99
  94.2 0.1 copy.48
  94.3 0.0 copy-done.3
  94.3 0.0 copy-done.4
  94.3 0.6 slice_add_fusion
  94.9 0.3 convolution_bitcast_fusion.1
  95.2 0.2 copy.49
  95.4 2.1 reshape.100
  97.5 1.0 copy.50
  98.5 0.9 convolution_bitcast_fusion
  99.4 0.2 copy.51
  99.6 1.6 multiply_bitcast_fusion
  101.2 4.0 %copy.53 = f32[192,32,64]{2,1,0:T(8,128)} copy(f32[192,32,64]{0,2,1:T(8,128)} %multiply_bitcast_fusion) | data formatting | bytes 3145728 | tf_op jit(solution)/shard_map/reshape | solution.py:160
  105.2 0.0 copy-start.1
  105.2 5.0 %convolution_convert_fusion.2 = bf16[192,32,64]{2,1,0:T(8,128)(2,1)} fusion(f32[192,32,64]{2,1,0:T(8,128)} %copy.53, bf16[192,64,64]{2,1,0:T(8,128)(2,1)S(1)} %copy.54), kind=kOutput, calls=%fused_computation.10 | convolution fusion | flops 302383104 | bytes 3932160 | tf_op jit(solution)/shard_map/tpk,tkn->tpn/dot_general | solution.py:163
  110.2 2.4 copy.55
  112.6 0.0 copy-done.1
  112.6 0.0 copy-start.2
  112.6 0.6 convolution_convert_fusion
  113.2 1.3 copy.68
  114.4 8.4 %all-to-all-start.2 = ((bf16[64,4,8,256]{3,2,1,0:T(8,128)(2,1)}), bf16[64,4,8,256]{3,2,1,0:T(8,128)(2,1)S(1)}, u32[]{:S(2)}, u32[]{:S(2)}) async-start(bf16[64,4,8,256]{3,2,1,0:T(8,128)(2,1)} %bitcast.52), calls=%async_computation.2 | async-start | bytes 2097152 | tf_op jit(solution)/shard_map/all_to_all | solution.py:193
  122.9 0.0 copy-done.2
  122.9 0.1 select_reduce_fusion
  123.0 0.1 broadcast_in_dim.18
  123.1 28.1 %all-to-all-done.2 = bf16[64,4,8,256]{3,2,1,0:T(8,128)(2,1)S(1)} async-done(((bf16[64,4,8,256]{3,2,1,0:T(8,128)(2,1)}), bf16[64,4,8,256]{3,2,1,0:T(8,128)(2,1)S(1)}, u32[]{:S(2)}, u32[]{:S(2)}) %all-to-all-start.2) | async-done | bytes 1048608 | tf_op jit(solution)/shard_map/all_to_all | solution.py:193
  151.2 0.8 broadcast_in_dim.19
  152.0 6.9 %all-to-all-start = ((s32[64,4,8,1]{2,1,3,0:T(4,128)}), s32[64,4,8,1]{2,1,3,0:T(4,128)S(1)}, u32[]{:S(2)}, u32[]{:S(2)}) async-start(s32[64,4,8,1]{2,1,3,0:T(4,128)} %broadcast_in_dim.19), calls=%async_computation | async-start | bytes 262144 | tf_op jit(solution)/shard_map/all_to_all | solution.py:200
  158.9 1.2 copy.65
  160.1 7.9 %all-to-all-done = s32[64,4,8,1]{2,1,3,0:T(4,128)S(1)} async-done(((s32[64,4,8,1]{2,1,3,0:T(4,128)}), s32[64,4,8,1]{2,1,3,0:T(4,128)S(1)}, u32[]{:S(2)}, u32[]{:S(2)}) %all-to-all-start) | async-done | bytes 8224 | tf_op jit(solution)/shard_map/all_to_all | solution.py:200
  168.0 9.4 %all-to-all-start.3 = ((bf16[1,256,8,256]{3,1,0,2:T(8,128)(2,1)}), bf16[1,256,8,256]{3,1,0,2:T(8,128)(2,1)S(1)}, u32[]{:S(2)}, u32[]{:S(2)}) async-start(bf16[1,256,8,256]{3,1,0,2:T(8,128)(2,1)} %copy.65), calls=%async_computation.3 | async-start | bytes 2097152 | tf_op jit(solution)/shard_map/all_to_all | solution.py:192
  177.4 0.7 copy.46
  178.1 28.0 %all-to-all-done.3 = bf16[1,256,8,256]{3,1,0,2:T(8,128)(2,1)S(1)} async-done(((bf16[1,256,8,256]{3,1,0,2:T(8,128)(2,1)}), bf16[1,256,8,256]{3,1,0,2:T(8,128)(2,1)S(1)}, u32[]{:S(2)}, u32[]{:S(2)}) %all-to-all-start.3) | async-done | bytes 1048608 | tf_op jit(solution)/shard_map/all_to_all | solution.py:192
  206.1 3.5 %all-to-all-start.1 = ((s32[1,256,8,1]{1,3,0,2:T(1,128)}), s32[1,256,8,1]{1,3,0,2:T(1,128)S(1)}, u32[]{:S(2)}, u32[]{:S(2)}) async-start(s32[1,256,8,1]{1,3,0,2:T(1,128)} %copy.46), calls=%async_computation.1 | async-start | bytes 16384 | tf_op jit(solution)/shard_map/all_to_all | solution.py:199
  209.6 0.6 copy.57
  210.3 6.8 %all-to-all-done.1 = s32[1,256,8,1]{1,3,0,2:T(1,128)S(1)} async-done(((s32[1,256,8,1]{1,3,0,2:T(1,128)}), s32[1,256,8,1]{1,3,0,2:T(1,128)S(1)}, u32[]{:S(2)}, u32[]{:S(2)}) %all-to-all-start.1) | async-done | bytes 8224 | tf_op jit(solution)/shard_map/all_to_all | solution.py:199
  217.1 1.6 fusion.9
  218.7 5.8 %copy.58 = bf16[4,4,8,256,8]{4,3,2,1,0:T(8,128)(2,1)} copy(bf16[4,4,8,256,8]{3,4,2,0,1:T(8,128)(2,1)S(1)} %fusion.9) | data formatting | bytes 1048576 | tf_op jit(solution)/shard_map/convert_element_type | solution.py:219
  224.4 12.8 %convert_element_type.43 = bf16[4,32,2048]{2,1,0:T(8,128)(2,1)S(1)} reshape(bf16[4,4,8,256,8]{4,3,2,1,0:T(8,128)(2,1)} %copy.58) | data formatting | bytes 1048576 | tf_op jit(solution)/shard_map/convert_element_type | solution.py:219
  237.3 4.2 %fusion.5 = bf16[4,1792,32]{1,2,0:T(8,128)(2,1)S(1)} fusion(bf16[2048,1792,1]{1,0,2:T(8,128)(2,1)} %bitcast.91, bf16[4,32,2048]{2,1,0:T(8,128)(2,1)S(1)} %convert_element_type.43), kind=kOutput, calls=%fused_computation.7 | convolution fusion | flops 939753472 | bytes 8323072 | tf_op jit(solution)/shard_map/pns,sb->pbn/dot_general | solution.py:220
  241.5 1.9 copy.59
  243.4 1.3 reshape.111
  244.8 22.6 %all_to_all.72 = bf16[64,2,1792]{2,1,0:T(2,128)(2,1)S(1)} all-to-all(bf16[64,2,1792]{2,1,0:T(2,128)(2,1)S(1)} %reshape.111), channel_id=1, replica_groups=mesh['occ'=8,'ao'=64] {'ao'}, dimensions={0} | all-to-all | bytes 917504 | tf_op jit(solution)/shard_map/all_to_all | solution.py:225
  267.4 1.0 reshape.112
  268.4 1.8 copy.72
  270.2 3.2 %all_to_all.66 = bf16[4,28,2048]{2,0,1:T(4,128)(2,1)S(1)} reshape(bf16[4,28,64,32]{3,2,0,1:T(8,128)(2,1)} %bitcast.95) | data formatting | bytes 917504 | tf_op jit(solution)/shard_map/all_to_all | solution.py:225
  273.4 4.4 %fusion.13 = f32[4,28,1792]{2,1,0:T(8,128)S(1)} fusion(bf16[2048,1792,1]{1,0,2:T(8,128)(2,1)} %bitcast.92, bf16[4,28,2048]{2,0,1:T(4,128)(2,1)S(1)} %all_to_all.66), kind=kOutput, calls=%fused_computation.17 | convolution fusion | flops 822083584 | bytes 8601600 | tf_op jit(solution)/shard_map/pbn,na->pba/dot_general | solution.py:223
  277.8 1.4 copy.63
  (2 shorter events, 0.0 us)
Async XLA Ops:
  0.0 3.0 %copy-start = (bf16[32,256]{1,0:T(8,128)(2,1)S(1)}, bf16[32,256]{1,0:T(8,128)(2,1)}, u32[]{:S(2)}) copy-start(bf16[32,256]{1,0:T(8,128)(2,1)} %param.12) | copy-start | bytes 49156
  11.3 83.1 %copy-start.3 = (s32[192,3]{0,1:T(4,128)S(1)}, s32[192,3]{0,1:T(4,128)}, u32[]{:S(2)}) copy-start(s32[192,3]{0,1:T(4,128)} %param.9) | copy-start | bytes 6916
  11.3 83.1 %copy-start.4 = (s32[192,1]{0,1:T(1,128)S(1)}, s32[192,1]{0,1:T(1,128)}, u32[]{:S(2)}) copy-start(s32[192,1]{0,1:T(1,128)} %param.10) | copy-start | bytes 2308
  105.2 7.4 %copy-start.1 = (s32[192]{0:T(256)S(1)}, s32[192]{0:T(256)}, u32[]{:S(2)}) copy-start(s32[192]{0:T(256)} %multiply_add_fusion.1) | copy-start | bytes 2308
  112.6 10.3 %copy-start.2 = (s32[192,1]{0,1:T(1,128)S(1)}, s32[192,1]{0,1:T(1,128)}, u32[]{:S(2)}) copy-start(s32[192,1]{0,1:T(1,128)} %get-tuple-element.13) | copy-start | bytes 2308
  114.4 36.7 %all-to-all-start.2 = ((bf16[64,4,8,256]{3,2,1,0:T(8,128)(2,1)}), bf16[64,4,8,256]{3,2,1,0:T(8,128)(2,1)S(1)}, u32[]{:S(2)}, u32[]{:S(2)}) async-start(bf16[64,4,8,256]{3,2,1,0:T(8,128)(2,1)} %bitcast.52), calls=%async_computation.2 | async-start | bytes 2097152 | tf_op jit(solution)/shard_map/all_to_all | solution.py:193
  152.0 16.1 %all-to-all-start = ((s32[64,4,8,1]{2,1,3,0:T(4,128)}), s32[64,4,8,1]{2,1,3,0:T(4,128)S(1)}, u32[]{:S(2)}, u32[]{:S(2)}) async-start(s32[64,4,8,1]{2,1,3,0:T(4,128)} %broadcast_in_dim.19), calls=%async_computation | async-start | bytes 262144 | tf_op jit(solution)/shard_map/all_to_all | solution.py:200
  168.0 38.0 %all-to-all-start.3 = ((bf16[1,256,8,256]{3,1,0,2:T(8,128)(2,1)}), bf16[1,256,8,256]{3,1,0,2:T(8,128)(2,1)S(1)}, u32[]{:S(2)}, u32[]{:S(2)}) async-start(bf16[1,256,8,256]{3,1,0,2:T(8,128)(2,1)} %copy.65), calls=%async_computation.3 | async-start | bytes 2097152 | tf_op jit(solution)/shard_map/all_to_all | solution.py:192
  206.1 11.0 %all-to-all-start.1 = ((s32[1,256,8,1]{1,3,0,2:T(1,128)}), s32[1,256,8,1]{1,3,0,2:T(1,128)S(1)}, u32[]{:S(2)}, u32[]{:S(2)}) async-start(s32[1,256,8,1]{1,3,0,2:T(1,128)} %copy.46), calls=%async_computation.1 | async-start | bytes 16384 | tf_op jit(solution)/shard_map/all_to_all | solution.py:199

commit v2 on v0

v2 whole, which is shorter than its diff:
```python
import jax
import jax.numpy as jnp
from jax import lax
from jax.experimental import pallas as pl
from jax.experimental.pallas import tpu as pltpu
from jax.sharding import PartitionSpec as P

NY, NX, NZ = 8, 4, 2
N_AO, N_OCC = 64, 8
TILES = 192
LANES = 256
CAP = 4
SLOTS = N_OCC * CAP
PAIRS = 32
P_LOC = PAIRS // N_OCC
NVIR = 1792
B_LOC = NVIR // N_AO
B_PAD = 32
CHUNK = 256
MESH = pl.DeviceIdType.MESH
F32, BF16, I32 = jnp.float32, jnp.bfloat16, jnp.int32


def remote(src, dst, send, recv, occ, ao):
    return pltpu.make_async_remote_copy(
        src_ref=src, dst_ref=dst, send_sem=send, recv_sem=recv,
        device_id=(occ, ao), device_id_type=MESH,
    )


def dot(a, b, dims=((1,), (0,))):
    return lax.dot_general(a, b, (dims, ((), ())), preferred_element_type=F32)


def iota(shape, dim):
    return lax.broadcasted_iota(I32, shape, dim)


def each(lo, hi, body, unroll=1):
    def step(k, carry):
        body(k)
        return carry

    lax.fori_loop(lo, hi, step, 0, unroll=unroll)


def kernel(
    ints_ref, owner_ref, blocks_ref, nuo_ref, pairs_ref, occ_ref, vir_ref,
    out_ref,
    cols, cols_f, vir, virp, flat, diag, expand, dens, part, s1, r1, meta, ids_o, sf, s2, r2, ids_s, ids_r,
    hot, hf, hb, vt, vs, vd, lhs,
    g_s, g_r, y_s, y_r, z_s, z_r, x_s, x_r, c_s, c_r, m_s, m_r, a_s, a_r, b_s, b_r, i_s, i_r, v_s, v_r,
):
    occ = lax.axis_index("occ")
    ao = lax.axis_index("ao")
    half = lax.rem(occ, 2)
    sibling = occ + 1 - 2 * half
    zl = lax.rem(ao, NZ)
    x = lax.rem(ao // NZ, NX)
    y = ao // (NZ * NX)

    def ao_of(yy, xx, zz):
        return (yy * NX + xx) * NZ + zz

    def ao_to(k):
        return lax.rem(ao + k, N_AO)

    def occ_to(k):
        return lax.rem(occ + k, N_OCC)

    barrier = pltpu.get_barrier_semaphore()

    def greet_ao(k):
        pl.semaphore_signal(barrier, inc=1, device_id=(occ, ao_to(k)), device_id_type=MESH)

    def greet_occ(k):
        pl.semaphore_signal(barrier, inc=1, device_id=(occ_to(k), ao), device_id_type=MESH)

    each(1, N_OCC, greet_occ)
    each(1, N_AO, greet_ao)

    pick = (iota((256, 128), 0) == jnp.broadcast_to(pairs_ref[...], (256, 128))).astype(F32).astype(BF16)
    sel = dot(occ_ref[...], pick)
    cols[ao] = jnp.where(iota((16, 128), 1) < 64, sel[:16], sel[16:]).astype(BF16)

    def padded(row, fill):
        return jnp.concatenate([row.astype(F32), jnp.full((1, LANES - TILES), fill, F32)], axis=1)

    owner = padded(owner_ref[...], -1.0)
    mu = blocks_ref[0:1]
    la = blocks_ref[1:2]
    rows = jnp.concatenate(
        [
            owner,
            padded((mu // 4) * 2 + mu % 2, -1.0),
            padded((mu // 2) % 2, 0.0),
            padded((la // 4) * 2 + la % 2, -1.0),
            padded((la // 2) % 2, 0.0),
            jnp.zeros((3, LANES), F32),
        ],
        axis=0,
    )
    upright = jnp.concatenate([rows, jnp.zeros((120, LANES), F32)], axis=0).T
    same = (upright[:, 0:1] == owner) & (iota((LANES, LANES), 0) < iota((LANES, LANES), 1))
    rank = jnp.sum(jnp.where(same, 1.0, 0.0), axis=0, keepdims=True)
    key = jnp.where(owner < 0.0, 256.0, rank * N_AO + owner)
    meta[occ] = jnp.concatenate(
        [key, padded(blocks_ref[2:3], 0.0), padded(nuo_ref[...], 0.0), jnp.zeros((5, LANES), F32)], axis=0
    )

    pl.semaphore_wait(barrier, N_AO + N_OCC - 2)

    def g_copy(k):
        return remote(cols.at[ao], cols.at[ao], g_s.at[k], g_r.at[k], occ, ao_to(k))

    def m_copy(k):
        return remote(meta.at[occ], meta.at[occ], m_s.at[k], m_r.at[k], occ_to(k), ao)

    def y_copy(k):
        return remote(
            vir_ref.at[half], vir.at[y, x, zl, half], y_s.at[k], y_r.at[k], occ, ao_of(lax.rem(y + k, NY), x, zl)
        )

    each(1, N_AO, lambda k: g_copy(k).start())
    each(1, N_OCC, lambda k: m_copy(k).start())
    each(1, NY, lambda k: y_copy(k).start())
    vir[y, x, zl, half] = vir_ref[half]

    def expansion(n):
        k = iota((1024, 128), 1) % 64
        p = n * 2 + iota((1024, 128), 1) // 64
        d = iota((1024, 128), 0) // 128
        hit = (iota((1024, 128), 0) % 32) == p
        left = hit & (d == (k % 32) // 4)
        right = hit & (d == (k % 4) * 2 + k // 32)
        expand[0, n] = jnp.where(left, 1.0, 0.0).astype(BF16)
        expand[1, n] = jnp.where(right, 1.0, 0.0).astype(BF16)

    each(0, 16, expansion)

    for kk in range(32):
        flat[kk * TILES:(kk + 1) * TILES] = ints_ref[:, kk * 128:(kk + 1) * 128].astype(F32)
    low = iota((32, 128), 1) < 64

    def place(t):
        block = flat[pl.ds(t, 32, stride=TILES), :]
        turned = pltpu.roll(block, 64, 1)
        zero = jnp.zeros_like(block)
        diag[t] = jnp.concatenate(
            [
                jnp.where(low, block, zero),
                jnp.where(low, turned, zero),
                jnp.where(low, zero, turned),
                jnp.where(low, zero, block),
            ],
            axis=0,
        ).astype(BF16)

    each(0, TILES, place, unroll=4)

    each(1, NY, lambda k: y_copy(k).wait())
    z_ref = vir.at[:, x, zl, half]
    z_copy = remote(z_ref, z_ref, z_s, z_r, occ, ao_of(y, x, 1 - zl))
    z_copy.start()

    each(1, N_AO, lambda k: g_copy(k).wait())
    cols_f[...] = cols[...].astype(F32).reshape(N_AO * 16, 128)
    table = jnp.concatenate(
        [cols_f[pl.ds(d, 128, stride=8), :].astype(BF16) for d in range(8)], axis=1
    )

    lane = iota((TILES, 1024), 1)

    def chosen(which):
        at = upright[:TILES, 1 + 2 * which:2 + 2 * which]
        part_of = upright[:TILES, 2 + 2 * which:3 + 2 * which]
        hot_rows = (iota((TILES, 128), 1).astype(F32) == at)
        got = dot(jnp.where(hot_rows, 1.0, 0.0).astype(BF16), table)
        keep = ((lane // 64) % 2).astype(F32) == part_of
        keep = keep & ((lane // 32) % 2 == which)
        return jnp.where(keep, got, 0.0).astype(BF16)

    left = chosen(0)
    right = chosen(1)
    for n in range(16):
        dens[n * TILES:(n + 1) * TILES] = dot(left, expand[0, n]) * dot(right, expand[1, n])

    def multiply(t):
        d = dens[pl.ds(t, 16, stride=TILES), :]
        hi = d.astype(BF16)
        lo = (d - hi.astype(F32)).astype(BF16)
        got = dot(jnp.concatenate([hi, lo], axis=0), diag[t])
        part[pl.ds(t, 16, stride=TILES), :] = got[:16] + got[16:]

    each(0, TILES, multiply, unroll=8)
    for n in range(16):
        s1[n // 2, :, (n % 2) * 128:(n % 2 + 1) * 128] = part[n * TILES:(n + 1) * TILES].astype(BF16)

    def a_copy(k):
        return remote(s1.at[occ_to(k)], r1.at[occ], a_s.at[k], a_r.at[k], occ_to(k), ao)

    each(1, N_OCC, lambda k: a_copy(k).start())
    r1[occ] = s1[occ]

    z_copy.wait()
    to_r, to_l, far = lax.rem(x + 1, NX), lax.rem(x + NX - 1, NX), lax.rem(x + 2, NX)

    def x_copy(n, block, lo, hi, to):
        ref = vir.at[lo:hi, block, :, half]
        return remote(ref, ref, x_s.at[n], x_r.at[n], occ, ao_of(y, to, zl))

    def c_copy(n, block):
        ref = vir.at[:, block, :, half]
        return remote(ref, ref, c_s.at[n], c_r.at[n], sibling, ao)

    x_copies = [
        x_copy(0, x, 0, NY, to_r),
        x_copy(1, x, 0, NY, to_l),
        x_copy(2, to_l, 0, NY // 2, to_r),
        x_copy(3, to_r, NY // 2, NY, to_l),
    ]
    c_copies = [c_copy(0, x), c_copy(1, to_l), c_copy(2, to_r), c_copy(3, far)]
    x_copies[0].start()
    x_copies[1].start()
    c_copies[0].start()

    each(1, N_OCC, lambda k: m_copy(k).wait())

    def sort(k):
        o = lax.rem(occ + N_OCC - k, N_OCC)

        @pl.when(k > 0)
        def _():
            a_copy(k).wait_recv()

        info = meta[o]
        hot_slots = jnp.where(
            iota((256, LANES), 0).astype(F32) == info[0:1], 1.0, 0.0
        ).astype(BF16)
        got = dot(hot_slots[:, :TILES], r1[o])
        for r in range(CAP):
            for n in range(2):
                sf[n, pl.ds(r * N_OCC + o, N_AO, stride=SLOTS), :] = got[r * 64:(r + 1) * 64, n * 128:(n + 1) * 128]
        names = dot(info.astype(BF16), hot_slots, ((1,), (1,)))
        ids_o[pl.ds(o, 1), :] = names[2:3] * 256.0 + names[1:2]

    each(0, N_OCC, sort)
    for n in range(2):
        s2[:, :, n * 128:(n + 1) * 128] = sf[n].astype(BF16).reshape(N_AO, SLOTS, 128)
    turned_ids = jnp.concatenate([ids_o[...], jnp.zeros((120, 256), F32)], axis=0).T
    wide = jnp.zeros((N_AO, 128), F32)
    for r in range(CAP):
        wide = wide + pltpu.roll(turned_ids[r * 64:(r + 1) * 64], r * N_OCC, 1)
    ids_s[...] = wide.reshape(N_AO, 1, 128)

    def b_copy(k):
        return remote(s2.at[ao_to(k)], r2.at[ao], b_s.at[k], b_r.at[k], occ, ao_to(k))

    def i_copy(k):
        return remote(ids_s.at[ao_to(k)], ids_r.at[ao], i_s.at[k], i_r.at[k], occ, ao_to(k))

    def start_b(k):
        i_copy(k).start()
        b_copy(k).start()

    each(1, N_AO, start_b)
    r2[ao] = s2[ao]
    ids_r[ao] = ids_s[ao]

    x_copies[0].wait_recv()
    x_copies[2].start()
    x_copies[1].wait_recv()
    x_copies[3].start()
    c_copies[1].start()
    c_copies[2].start()
    x_copies[2].wait_recv()
    x_copies[3].wait_recv()
    c_copies[3].start()
    for n in range(4):
        c_copies[n].wait_recv()

    order = jnp.where(
        iota((256, 256), 1) == (iota((256, 256), 0) % 32) * 8 + iota((256, 256), 0) // 32, 1.0, 0.0
    ).astype(BF16)

    def chunk(n):
        return pl.ds(pl.multiple_of(n * CHUNK, CHUNK), CHUNK)

    def reorder(n):
        for j in range(NY):
            got = dot(order, vir[j, :, :, :, :, chunk(n)].reshape(256, CHUNK)).astype(BF16)
            for si in range(8):
                virp[si * 256 + j * 32:si * 256 + (j + 1) * 32, chunk(n)] = got[si * 32:(si + 1) * 32]

    each(0, NVIR // CHUNK, reorder)

    def end_b(k):
        i_copy(k).wait()
        b_copy(k).wait()

    each(1, N_AO, end_b)

    def mark(s):
        names = jnp.broadcast_to(ids_r[s], (SLOTS, 128))
        name = jnp.sum(jnp.where(iota((SLOTS, 128), 0) == iota((SLOTS, 128), 1), names, 0.0), axis=1, keepdims=True)
        hot[s] = jnp.where(iota((SLOTS, 1024), 1).astype(F32) == name, 1.0, 0.0).astype(BF16)

    each(0, N_AO, mark, unroll=2)
    got_rows = r2[...].reshape(N_AO * SLOTS, 256)
    for n in range(4):
        total = dot(got_rows, hot[:, :, n * 256:(n + 1) * 256].reshape(N_AO * SLOTS, 256), ((0,), (0,)))
        hf[2 * n] = total[:, :128]
        hf[2 * n + 1] = total[:, 128:]
    for si in range(8):
        for m in range(2):
            hb[:, si * 256 + m * 128:si * 256 + (m + 1) * 128] = jnp.concatenate(
                [hf[2 * n + m, pl.ds(p * 64 + si, 8, stride=8), :] for p in range(P_LOC) for n in range(4)], axis=0
            ).astype(BF16)

    def first(n):
        rows_v = dot(hb[...], virp[:, chunk(n)]).astype(BF16).astype(F32)
        vt[chunk(n)] = rows_v.T

    each(0, NVIR // CHUNK, first)
    vt[NVIR:] = jnp.zeros((8, 128), F32)
    for s in range(N_AO):
        vs[s] = vt[s * B_LOC:s * B_LOC + B_PAD].astype(BF16)

    def v_copy(k):
        return remote(vs.at[ao_to(k)], vd.at[ao], v_s.at[k], v_r.at[k], occ, ao_to(k))

    each(1, N_AO, lambda k: v_copy(k).start())
    vd[ao] = vs[ao]
    each(1, N_AO, lambda k: v_copy(k).wait())

    quarter = iota((B_PAD, 128), 1) // 32

    def regroup(g):
        got = [vd[4 * g + s].astype(F32) for s in range(4)]
        for p in range(P_LOC):
            mixed = jnp.zeros((B_PAD, 128), F32)
            for s in range(4):
                shift = ((s - p) % 4) * 32
                piece = pltpu.roll(got[s], shift, 1) if shift else got[s]
                mixed = jnp.where(quarter == s, piece, mixed)
            lhs[g // 2, p * B_PAD:(p + 1) * B_PAD, pl.ds(pl.multiple_of((g % 2) * 128, 128), 128)] = mixed.astype(BF16)

    each(0, N_AO // 4, regroup, unroll=2)

    def second(n):
        total = jnp.zeros((P_LOC * B_PAD, CHUNK), F32)
        for j in range(NY):
            total = total + dot(lhs[j], vir[j, :, :, :, :, chunk(n)].reshape(256, CHUNK))
        for p in range(P_LOC):
            out_ref[p, :, chunk(n)] = total[p * B_PAD:p * B_PAD + B_LOC]

    each(0, NVIR // CHUNK, second)

    each(1, N_OCC, lambda k: a_copy(k).wait_send())
    for n in range(4):
        x_copies[n].wait_send()
        c_copies[n].wait_send()


def shards(integrals, tile_owner, tile_blocks, nu_offset, pair_list, occ_coef, vir_coef):
    pairs = jnp.tile(pair_list.T.reshape(1, 2 * PAIRS), (1, 2))
    dma = pltpu.SemaphoreType.DMA
    vmem = pltpu.VMEM
    return pl.pallas_call(
        kernel,
        out_shape=jax.ShapeDtypeStruct((P_LOC, B_LOC, NVIR), F32),
        in_specs=[pl.BlockSpec(memory_space=pltpu.VMEM)] * 7,
        out_specs=pl.BlockSpec(memory_space=pltpu.VMEM),
        scratch_shapes=[
            vmem((N_AO, 16, 128), BF16),
            vmem((N_AO * 16, 128), F32),
            vmem((NY, NX, NZ, 2, 16, NVIR), BF16),
            vmem((N_AO * 32, NVIR), BF16),
            vmem((32 * TILES, 128), F32),
            vmem((TILES, 128, 128), BF16),
            vmem((2, 16, 1024, 128), BF16),
            vmem((16 * TILES, 128), F32),
            vmem((16 * TILES, 128), F32),
            vmem((N_OCC, TILES, 256), BF16),
            vmem((N_OCC, TILES, 256), BF16),
            vmem((N_OCC, 8, LANES), F32),
            vmem((N_OCC, 256), F32),
            vmem((2, N_AO * SLOTS, 128), F32),
            vmem((N_AO, SLOTS, 256), BF16),
            vmem((N_AO, SLOTS, 256), BF16),
            vmem((N_AO, 1, 128), F32),
            vmem((N_AO, 1, 128), F32),
            vmem((N_AO, SLOTS, 1024), BF16),
            vmem((8, 256, 128), F32),
            vmem((128, 2048), BF16),
            vmem((NVIR + 8, 128), F32),
            vmem((N_AO, B_PAD, 128), BF16),
            vmem((N_AO, B_PAD, 128), BF16),
            vmem((NY, 128, 256), BF16),
            dma((N_AO,)), dma((N_AO,)), dma((NY,)), dma((NY,)), dma, dma,
            dma((4,)), dma((4,)), dma((4,)), dma((4,)), dma((N_OCC,)), dma((N_OCC,)), dma((N_OCC,)), dma((N_OCC,)),
            dma((N_AO,)), dma((N_AO,)), dma((N_AO,)), dma((N_AO,)), dma((N_AO,)), dma((N_AO,)),
        ],
        compiler_params=pltpu.CompilerParams(
            collective_id=0, has_side_effects=True, vmem_limit_bytes=60 * 1024 * 1024
        ),
    )(
        integrals, tile_owner.T, tile_blocks.T, nu_offset.T, pairs, occ_coef,
        vir_coef.reshape(2, 16, NVIR),
    )


def solution(mesh):
    placed = (
        P(("occ", "ao"), None),
        P(("occ", "ao"), None),
        P(("occ", "ao"), None),
        P(("occ", "ao"), None),
        P(),
        P("ao", None),
        P("ao", None),
    )
    return jax.shard_map(
        shards, mesh=mesh, in_specs=placed, out_specs=P("occ", "ao", None), check_vma=False
    )
```

time: 688 us -> 131 us (0.19)
  the two profiles are of different devices: /device:TPU:56 before, /device:TPU:135 now
where the time goes in v2:
time: 131 us; the launch traced here: 130 us
  Pallas kernels  126 us (96%)
  local copies, waits for them, and re-layouts  3.94 us (3%)
    pallas_call x1, Pallas kernels, shards(): pl.pallas_call(kernel, out_shape=jax.ShapeDtypeStruct((P_LOC, B_LOC, NVIR...  126 us

profile of v2, /device:TPU:135, one launch (start us, length us, event | category | flops | bytes accessed | tf_op | source)
XLA Modules:
  0.0 130.3 jit_solution(6260287720974853525)
XLA Ops:
  0.0 0.8 tile.10
  0.8 0.6 tile.12.pairs_ref
  1.4 126.4 %shard_map.73 = f32[4,28,1792]{2,1,0:T(8,128)} custom-call(bf16[192,4096]{1,0:T(8,128)(2,1)} %ints_ref.1, s32[1,192]{1,0:T(1,128)} %bitcast.7, s32[3,192]{1,0:T(4,128)} %bitcast.6, s32[1,192]{1,0:T(1,128)} %bitcast.8, s32[1,128]{1,0:T(1,128)} %tile.12.pairs_ref, bf16[32,256]{1,0:T(8,128)(2,1)} %occ_ref.1, bf16[2,16,1792]{2,1,0:T(8,128)(2,1)} %bitcast.5), custom_call_target="tpu_custom_call" | custom-call | tf_op jit(solution)/shard_map/pallas_call | solution.py:369
  127.8 2.6 %copy.8 = f32[4,28,1792]{2,0,1:T(4,128)} copy(f32[4,28,1792]{2,1,0:T(8,128)} %shard_map.73) | data formatting | bytes 1605632 | tf_op jit(solution)/shard_map/pallas_call | solution.py:369
  (1 shorter events, 0.0 us)

commit v3 on v2

v3 whole, which is shorter than its diff:
```python
import jax
import jax.numpy as jnp
from jax import lax
from jax.experimental import pallas as pl
from jax.experimental.pallas import tpu as pltpu
from jax.sharding import PartitionSpec as P

NY, NX, NZ = 8, 4, 2
N_AO, N_OCC = 64, 8
TILES = 192
LANES = 256
CAP = 4
SLOTS = N_OCC * CAP
PAIRS = 32
P_LOC = PAIRS // N_OCC
NVIR = 1792
B_LOC = NVIR // N_AO
B_PAD = 32
CHUNK = 256
MESH = pl.DeviceIdType.MESH
F32, BF16, I32 = jnp.float32, jnp.bfloat16, jnp.int32


def remote(src, dst, send, recv, occ, ao):
    return pltpu.make_async_remote_copy(
        src_ref=src, dst_ref=dst, send_sem=send, recv_sem=recv,
        device_id=(occ, ao), device_id_type=MESH,
    )


def dot(a, b, dims=((1,), (0,))):
    return lax.dot_general(a, b, (dims, ((), ())), preferred_element_type=F32)


def iota(shape, dim):
    return lax.broadcasted_iota(I32, shape, dim)


def each(lo, hi, body, unroll=1):
    def step(k, carry):
        body(k)
        return carry

    lax.fori_loop(lo, hi, step, 0, unroll=unroll)


def kernel(
    ints_ref, owner_ref, blocks_ref, nuo_ref, pairs_ref, occ_ref, vir_ref,
    out_ref,
    cols, cols_f, vir, virp, flat, diag, expand, dens, part, s1, r1, meta, ids_o, sf, s2, r2, ids_s, ids_r,
    hot, hf, hb, vt, vs, vd, lhs, acc, places,
    g_s, g_r, y_s, y_r, z_s, z_r, x_s, x_r, c_s, c_r, m_s, m_r, a_s, a_r, b_s, b_r, i_s, i_r, v_s, v_r,
):
    occ = lax.axis_index("occ")
    ao = lax.axis_index("ao")
    half = lax.rem(occ, 2)
    sibling = occ + 1 - 2 * half
    zl = lax.rem(ao, NZ)
    x = lax.rem(ao // NZ, NX)
    y = ao // (NZ * NX)

    def ao_of(yy, xx, zz):
        return (yy * NX + xx) * NZ + zz

    xz = lax.rem(ao, 8)

    def wrap(t, n):
        return jnp.where(t >= n, t - n, t)

    Y_ORDER = (0, 1, 7, 2, 6, 3, 5, 4)

    def to_peers(body):
        for dy in Y_ORDER:
            base = wrap(y + dy, NY) * 8
            each(1 if dy == 0 else 0, 8, lambda q: body(dy * 8 + q, base + wrap(xz + q, 8)))

    OCC_ORDER = (1, 2, 3, 6, 7, 4, 5)

    def occ_to(k):
        return wrap(occ // 2 + k // 2, 4) * 2 + (half + k % 2) % 2

    def occ_from(k):
        return wrap(occ // 2 + 4 - k // 2, 4) * 2 + (half + k % 2) % 2

    def to_occ_peers(body):
        for k in OCC_ORDER:
            body(k, occ_to(k))

    barrier = pltpu.get_barrier_semaphore()

    to_occ_peers(
        lambda k, o: pl.semaphore_signal(barrier, inc=1, device_id=(o, ao), device_id_type=MESH)
    )
    to_peers(lambda k, a: pl.semaphore_signal(barrier, inc=1, device_id=(occ, a), device_id_type=MESH))
    ao_z = ao_of(y, x, 1 - zl)
    up, down = wrap(occ + 2 * zl, N_OCC), wrap(occ + 6 * (1 - zl), N_OCC)
    pl.semaphore_signal(
        barrier, inc=1, device_id=(wrap(occ + 6 - 4 * zl, N_OCC), ao_z), device_id_type=MESH
    )

    pick = (iota((256, 128), 0) == jnp.broadcast_to(pairs_ref[...], (256, 128))).astype(F32).astype(BF16)
    sel = dot(occ_ref[...], pick)
    cols[ao] = jnp.where(iota((16, 128), 1) < 64, sel[:16], sel[16:]).astype(BF16)

    def padded(row, fill):
        return jnp.concatenate([row.astype(F32), jnp.full((1, LANES - TILES), fill, F32)], axis=1)

    owner = padded(owner_ref[...], -1.0)
    mu = blocks_ref[0:1]
    la = blocks_ref[1:2]
    rows = jnp.concatenate(
        [
            owner,
            padded((mu // 4) * 2 + mu % 2, -1.0),
            padded((mu // 2) % 2, 0.0),
            padded((la // 4) * 2 + la % 2, -1.0),
            padded((la // 2) % 2, 0.0),
            jnp.zeros((3, LANES), F32),
        ],
        axis=0,
    )
    upright = jnp.concatenate([rows, jnp.zeros((120, LANES), F32)], axis=0).T
    same = (upright[:, 0:1] == owner) & (iota((LANES, LANES), 0) < iota((LANES, LANES), 1))
    rank = jnp.sum(jnp.where(same, 1.0, 0.0), axis=0, keepdims=True)
    key = jnp.where(owner < 0.0, 256.0, rank * N_AO + owner)
    meta[occ] = jnp.concatenate(
        [key, padded(blocks_ref[2:3], 0.0), padded(nuo_ref[...], 0.0), jnp.zeros((5, LANES), F32)], axis=0
    )

    def expansion(n):
        k = iota((256, 128), 1) % 64
        p = n * 2 + iota((256, 128), 1) // 64
        d = iota((256, 128), 0) // 32
        hit = (iota((256, 128), 0) % 32) == p
        left = hit & (d == (k % 32) // 4)
        right = hit & (d == (k % 4) * 2 + k // 32)
        expand[0, n] = jnp.where(left, 1.0, 0.0).astype(BF16)
        expand[1, n] = jnp.where(right, 1.0, 0.0).astype(BF16)

    each(0, 16, expansion)

    for kk in range(32):
        flat[kk * TILES:(kk + 1) * TILES] = ints_ref[:, kk * 128:(kk + 1) * 128].astype(F32)
    low = iota((32, 128), 1) < 64

    def place(t):
        block = flat[pl.ds(t, 32, stride=TILES), :]
        turned = pltpu.roll(block, 64, 1)
        zero = jnp.zeros_like(block)
        diag[t] = jnp.concatenate(
            [
                jnp.where(low, block, zero),
                jnp.where(low, turned, zero),
                jnp.where(low, zero, turned),
                jnp.where(low, zero, block),
            ],
            axis=0,
        ).astype(BF16)

    each(0, TILES, place, unroll=4)

    pl.semaphore_wait(barrier, N_AO + N_OCC - 1)

    def g_copy(k, a=0):
        return remote(cols.at[ao], cols.at[ao], g_s.at[k], g_r.at[k], occ, a)

    def m_copy(k, o=0):
        return remote(meta.at[occ], meta.at[occ], m_s.at[k], m_r.at[k], o, ao)

    def y_copy(k):
        return remote(
            vir_ref.at[half], vir.at[y, x, zl, half], y_s.at[k], y_r.at[k], occ, ao_of(wrap(y + k, NY), x, zl)
        )

    to_peers(lambda k, a: g_copy(k, a).start())
    to_occ_peers(lambda k, o: m_copy(k, o).start())
    vir[y, x, zl, half] = vir_ref[half]

    each(1, N_AO, lambda k: g_copy(k).wait())
    each(1, NY, lambda k: y_copy(k).start())
    cols_f[...] = cols[...].astype(F32).reshape(N_AO * 16, 128)
    table = jnp.concatenate(
        [cols_f[pl.ds(d, 128, stride=8), :].astype(BF16) for d in range(8)], axis=1
    )

    lane = iota((TILES, 1024), 1)

    def chosen(which):
        at = upright[:TILES, 1 + 2 * which:2 + 2 * which]
        part_of = upright[:TILES, 2 + 2 * which:3 + 2 * which]
        hot_rows = (iota((TILES, 128), 1).astype(F32) == at)
        got = dot(jnp.where(hot_rows, 1.0, 0.0).astype(BF16), table)
        keep = ((lane // 64) % 2).astype(F32) == part_of
        keep = keep & ((lane // 32) % 2 == which)
        got = jnp.where(keep, got, 0.0)
        folded = []
        for g in range(2):
            total = jnp.zeros((TILES, 128), F32)
            for d in range(4):
                piece = got[:, (g * 4 + d) * 128:(g * 4 + d + 1) * 128]
                piece = piece + pltpu.roll(piece, 64, 1)
                piece = piece + pltpu.roll(piece, 32, 1)
                total = jnp.where(iota((TILES, 128), 1) // 32 == d, piece, total)
            folded.append(total)
        return jnp.concatenate(folded, axis=1).astype(BF16)

    left = chosen(0)
    right = chosen(1)
    for n in range(16):
        dens[n * TILES:(n + 1) * TILES] = dot(left, expand[0, n]) * dot(right, expand[1, n])

    def multiply(t):
        d = dens[pl.ds(t, 16, stride=TILES), :]
        hi = d.astype(BF16)
        lo = (d - hi.astype(F32)).astype(BF16)
        got = dot(jnp.concatenate([hi, lo], axis=0), diag[t])
        part[pl.ds(t, 16, stride=TILES), :] = got[:16] + got[16:]

    each(0, TILES, multiply, unroll=8)
    def a_copy(n, k, o=0):
        return remote(s1.at[n, o], r1.at[n, occ], a_s.at[n, k], a_r.at[n, k], o, ao)

    for n in range(2):
        for o in range(N_OCC):
            at = (2 * o + n) * TILES
            s1[n, o] = part[at:at + TILES].astype(BF16)
        to_occ_peers(lambda k, o: a_copy(n, k, o).start())
        r1[n, occ] = s1[n, occ]

    each(1, NY, lambda k: y_copy(k).wait())
    to_r, to_l = wrap(x + 1, NX), wrap(x + NX - 1, NX)

    def x_copy(n, block, lo, hi, to):
        ref = vir.at[lo:hi, block, zl, half]
        return remote(ref, ref, x_s.at[n], x_r.at[n], occ, ao_of(y, to, zl))

    x_near, x_far = [], []
    for h in range(2):
        lo, hi = h * 4, h * 4 + 4
        x_near.append((x_copy(4 * h, x, lo, hi, to_r), x_copy(4 * h + 1, x, lo, hi, to_l)))
        x_far.append((x_copy(4 * h + 2, to_l, lo, lo + 2, to_r), x_copy(4 * h + 3, to_r, lo + 2, hi, to_l)))
    for h in range(2):
        for copy in x_near[h]:
            copy.start()
    to_occ_peers(lambda k, o: m_copy(k, o).wait())
    for h in range(2):
        for i in range(2):
            x_near[h][i].wait_recv()
            x_far[h][i].start()

    def z_copy(n):
        ref = vir.at[n * 4:n * 4 + 4, :, zl, half]
        return remote(ref, ref, z_s.at[n], z_r.at[n], (up, down)[n], ao_z)

    def c_copy(n, lo, hi, zz):
        ref = vir.at[lo:hi, :, zz, half]
        return remote(ref, ref, c_s.at[n], c_r.at[n], sibling, ao)

    z_copies = [z_copy(0), z_copy(1)]
    c_copies = [c_copy(0, 0, NY, zl), c_copy(1, 0, 4, 1 - zl), c_copy(2, 4, NY, 1 - zl)]

    def sort(n):
        for k in (0,) + OCC_ORDER:
            o = occ_from(k)
            if k > 0:
                a_copy(n, k).wait_recv()
            if n == 0:
                info = meta[o]
                hot_slots = jnp.where(
                    iota((256, LANES), 0).astype(F32) == info[0:1], 1.0, 0.0
                ).astype(BF16)
                places[o] = hot_slots
                names = dot(info.astype(BF16), hot_slots, ((1,), (1,)))
                ids_o[pl.ds(o, 1), :] = names[2:3] * 256.0 + names[1:2]
            else:
                hot_slots = places[o]
            got = dot(hot_slots[:, :TILES], r1[n, o])
            for r in range(CAP):
                sf[n, pl.ds(r * N_OCC + o, N_AO, stride=SLOTS), :] = got[r * 64:(r + 1) * 64]
        s2[n] = sf[n].astype(BF16).reshape(N_AO, SLOTS, 128)

    def b_copy(n, k, a=0):
        return remote(s2.at[n, a], r2.at[n, ao], b_s.at[n, k], b_r.at[n, k], occ, a)

    def i_copy(k, a=0):
        return remote(ids_s.at[a], ids_r.at[ao], i_s.at[k], i_r.at[k], occ, a)

    def start_first(k, a):
        i_copy(k, a).start()
        b_copy(0, k, a).start()

    def end_first(k):
        i_copy(k).wait()
        b_copy(0, k).wait()

    sort(0)
    turned_ids = jnp.concatenate([ids_o[...], jnp.zeros((120, 256), F32)], axis=0).T
    wide = jnp.zeros((N_AO, 128), F32)
    for r in range(CAP):
        wide = wide + pltpu.roll(turned_ids[r * 64:(r + 1) * 64], r * N_OCC, 1)
    ids_s[...] = wide.reshape(N_AO, 1, 128)
    to_peers(start_first)
    r2[0, ao] = s2[0, ao]
    ids_r[ao] = ids_s[ao]
    for h in range(2):
        for copy in x_far[h]:
            copy.wait_recv()
    for copy in z_copies:
        copy.start()
    c_copies[0].start()
    sort(1)
    to_peers(lambda k, a: b_copy(1, k, a).start())
    r2[1, ao] = s2[1, ao]

    def mark(s):
        names = jnp.broadcast_to(ids_r[s], (SLOTS, 128))
        name = jnp.sum(jnp.where(iota((SLOTS, 128), 0) == iota((SLOTS, 128), 1), names, 0.0), axis=1, keepdims=True)
        hot[s] = jnp.where(iota((SLOTS, 1024), 1).astype(F32) == name, 1.0, 0.0).astype(BF16)

    def collect(n):
        got_rows = r2[n].reshape(N_AO * SLOTS, 128)
        for m in range(4):
            total = dot(got_rows, hot[:, :, m * 256:(m + 1) * 256].reshape(N_AO * SLOTS, 256), ((0,), (0,)))
            hf[2 * m, n * 128:(n + 1) * 128] = total[:, :128]
            hf[2 * m + 1, n * 128:(n + 1) * 128] = total[:, 128:]

    each(1, N_AO, end_first)
    each(0, N_AO, mark, unroll=2)
    collect(0)
    for n in range(2):
        z_copies[n].wait_recv()
        c_copies[n + 1].start()
    each(1, N_AO, lambda k: b_copy(1, k).wait())
    collect(1)
    for copy in c_copies:
        copy.wait_recv()

    order = jnp.where(
        iota((256, 256), 1) == (iota((256, 256), 0) % 32) * 8 + iota((256, 256), 0) // 32, 1.0, 0.0
    ).astype(BF16)

    def chunk(n):
        return pl.ds(pl.multiple_of(n * CHUNK, CHUNK), CHUNK)

    def reorder(n):
        for j in range(NY):
            got = dot(order, vir[j, :, :, :, :, chunk(n)].reshape(256, CHUNK)).astype(BF16)
            for si in range(8):
                virp[si * 256 + j * 32:si * 256 + (j + 1) * 32, chunk(n)] = got[si * 32:(si + 1) * 32]

    each(0, NVIR // CHUNK, reorder)

    for si in range(8):
        for m in range(2):
            hb[:, si * 256 + m * 128:si * 256 + (m + 1) * 128] = jnp.concatenate(
                [hf[2 * n + m, pl.ds(p * 64 + si, 8, stride=8), :] for p in range(P_LOC) for n in range(4)], axis=0
            ).astype(BF16)

    def v_copy(k, a=0):
        return remote(vs.at[a], vd.at[ao], v_s.at[k], v_r.at[k], occ, a)

    def first(n):
        rows_v = dot(hb[...], virp[:, chunk(n)]).astype(BF16).astype(F32)
        vt[chunk(n)] = rows_v.T

    each(0, NVIR // CHUNK, first)
    vt[NVIR:] = jnp.zeros((8, 128), F32)
    for s in range(N_AO):
        vs[s] = vt[s * B_LOC:s * B_LOC + B_PAD].astype(BF16)
    to_peers(lambda k, a: v_copy(k, a).start())
    vd[ao] = vs[ao]

    quarter = iota((B_PAD, 128), 1) // 32

    def second(dy):
        sy = wrap(y + NY - dy, NY)
        each(1 if dy == 0 else 0, 8, lambda q: v_copy(dy * 8 + q).wait())
        for g in range(2):
            got = [vd[sy * 8 + 4 * g + s].astype(F32) for s in range(4)]
            for p in range(P_LOC):
                mixed = jnp.zeros((B_PAD, 128), F32)
                for s in range(4):
                    shift = ((s - p) % 4) * 32
                    piece = pltpu.roll(got[s], shift, 1) if shift else got[s]
                    mixed = jnp.where(quarter == s, piece, mixed)
                lhs[p * B_PAD:(p + 1) * B_PAD, g * 128:(g + 1) * 128] = mixed.astype(BF16)

        acc[...] += dot(lhs[...], vir[sy].reshape(256, NVIR))

    acc[...] = jnp.zeros_like(acc)
    for dy in Y_ORDER:
        second(dy)
    for p in range(P_LOC):
        out_ref[p] = acc[p * B_PAD:p * B_PAD + B_LOC]

    for n in range(2):
        each(1, N_OCC, lambda k: a_copy(n, k).wait_send())
    for copy in x_near[0] + x_near[1] + x_far[0] + x_far[1] + tuple(z_copies) + tuple(c_copies):
        copy.wait_send()


def shards(integrals, tile_owner, tile_blocks, nu_offset, pair_list, occ_coef, vir_coef):
    pairs = jnp.tile(pair_list.T.reshape(1, 2 * PAIRS), (1, 2))
    dma = pltpu.SemaphoreType.DMA
    vmem = pltpu.VMEM
    return pl.pallas_call(
        kernel,
        out_shape=jax.ShapeDtypeStruct((P_LOC, B_LOC, NVIR), F32),
        in_specs=[pl.BlockSpec(memory_space=pltpu.VMEM)] * 7,
        out_specs=pl.BlockSpec(memory_space=pltpu.VMEM),
        scratch_shapes=[
            vmem((N_AO, 16, 128), BF16),
            vmem((N_AO * 16, 128), F32),
            vmem((NY, NX, NZ, 2, 16, NVIR), BF16),
            vmem((N_AO * 32, NVIR), BF16),
            vmem((32 * TILES, 128), F32),
            vmem((TILES, 128, 128), BF16),
            vmem((2, 16, 256, 128), BF16),
            vmem((16 * TILES, 128), F32),
            vmem((16 * TILES, 128), F32),
            vmem((2, N_OCC, TILES, 128), BF16),
            vmem((2, N_OCC, TILES, 128), BF16),
            vmem((N_OCC, 8, LANES), F32),
            vmem((N_OCC, 256), F32),
            vmem((2, N_AO * SLOTS, 128), F32),
            vmem((2, N_AO, SLOTS, 128), BF16),
            vmem((2, N_AO, SLOTS, 128), BF16),
            vmem((N_AO, 1, 128), F32),
            vmem((N_AO, 1, 128), F32),
            vmem((N_AO, SLOTS, 1024), BF16),
            vmem((8, 256, 128), F32),
            vmem((128, 2048), BF16),
            vmem((NVIR + 8, 128), F32),
            vmem((N_AO, B_PAD, 128), BF16),
            vmem((N_AO, B_PAD, 128), BF16),
            vmem((128, 256), BF16),
            vmem((128, NVIR), F32),
            vmem((N_OCC, 256, LANES), BF16),
            dma((N_AO,)), dma((N_AO,)), dma((NY,)), dma((NY,)), dma((2,)), dma((2,)),
            dma((8,)), dma((8,)), dma((3,)), dma((3,)), dma((N_OCC,)), dma((N_OCC,)),
            dma((2, N_OCC)), dma((2, N_OCC)), dma((2, N_AO)), dma((2, N_AO)),
            dma((N_AO,)), dma((N_AO,)), dma((N_AO,)), dma((N_AO,)),
        ],
        compiler_params=pltpu.CompilerParams(
            collective_id=0, has_side_effects=True, vmem_limit_bytes=60 * 1024 * 1024
        ),
    )(
        integrals, tile_owner.T, tile_blocks.T, nu_offset.T, pairs, occ_coef,
        vir_coef.reshape(2, 16, NVIR),
    )


def solution(mesh):
    placed = (
        P(("occ", "ao"), None),
        P(("occ", "ao"), None),
        P(("occ", "ao"), None),
        P(("occ", "ao"), None),
        P(),
        P("ao", None),
        P("ao", None),
    )
    return jax.shard_map(
        shards, mesh=mesh, in_specs=placed, out_specs=P("occ", "ao", None), check_vma=False
    )
```

time: 131 us -> 122 us (0.931)
  the two profiles are of different devices: /device:TPU:135 before, /device:TPU:56 now
where the time goes in v3:
time: 122 us; the launch traced here: 121 us
  Pallas kernels  117 us (96%)
  local copies, waits for them, and re-layouts  3.94 us (3%)
    pallas_call x1, Pallas kernels, shards(): pl.pallas_call(kernel, out_shape=jax.ShapeDtypeStruct((P_LOC, B_LOC, NVIR...  117 us
    pallas_call x1, local copies, waits for them, and re-layouts, shards(): pl.pallas_call(kernel, out_shape=jax.ShapeDtypeStruct((P_LOC, B_LOC, NVIR...  2.58 us

profile of v3, /device:TPU:56, one launch (start us, length us, event | category | flops | bytes accessed | tf_op | source)
XLA Modules:
  0.0 120.7 jit_solution(9717236576111596494)
XLA Ops:
  0.0 0.8 tile.10
  0.8 0.6 tile.12.pairs_ref
  1.4 116.7 %shard_map.73 = f32[4,28,1792]{2,1,0:T(8,128)} custom-call(bf16[192,4096]{1,0:T(8,128)(2,1)} %ints_ref.1, s32[1,192]{1,0:T(1,128)} %bitcast.7, s32[3,192]{1,0:T(4,128)} %bitcast.6, s32[1,192]{1,0:T(1,128)} %bitcast.8, s32[1,128]{1,0:T(1,128)} %tile.12.pairs_ref, bf16[32,256]{1,0:T(8,128)(2,1)} %occ_ref.1, bf16[2,16,1792]{2,1,0:T(8,128)(2,1)} %bitcast.5), custom_call_target="tpu_custom_call" | custom-call | tf_op jit(solution)/shard_map/pallas_call | solution.py:406
  118.1 2.6 %copy.8 = f32[4,28,1792]{2,0,1:T(4,128)} copy(f32[4,28,1792]{2,1,0:T(8,128)} %shard_map.73) | data formatting | bytes 1605632 | tf_op jit(solution)/shard_map/pallas_call | solution.py:406
  (1 shorter events, 0.0 us)

commit v4 on v3

--- a/solution.py
+++ b/solution.py
@@ -93,9 +93,9 @@
     )
     to_peers(lambda k, a: pl.semaphore_signal(barrier, inc=1, device_id=(occ, a), device_id_type=MESH))
     ao_z = ao_of(y, x, 1 - zl)
-    up, down = wrap(occ + 2 * zl, N_OCC), wrap(occ + 6 * (1 - zl), N_OCC)
+    outer = wrap(occ + 6 - 4 * zl, N_OCC)
     pl.semaphore_signal(
-        barrier, inc=1, device_id=(wrap(occ + 6 - 4 * zl, N_OCC), ao_z), device_id_type=MESH
+        barrier, inc=1, device_id=(outer, ao_z), device_id_type=MESH
     )
 
     pick = (iota((256, 128), 0) == jnp.broadcast_to(pairs_ref[...], (256, 128))).astype(F32).astype(BF16)
@@ -123,8 +123,10 @@
     same = (upright[:, 0:1] == owner) & (iota((LANES, LANES), 0) < iota((LANES, LANES), 1))
     rank = jnp.sum(jnp.where(same, 1.0, 0.0), axis=0, keepdims=True)
     key = jnp.where(owner < 0.0, 256.0, rank * N_AO + owner)
+    shell = blocks_ref[2:3]
+    shell = ((shell // 4) % 2) * 128 + (shell // 8) * 4 + shell % 4
     meta[occ] = jnp.concatenate(
-        [key, padded(blocks_ref[2:3], 0.0), padded(nuo_ref[...], 0.0), jnp.zeros((5, LANES), F32)], axis=0
+        [key, padded(shell, 0.0), padded(nuo_ref[...], 0.0), jnp.zeros((5, LANES), F32)], axis=0
     )
 
     def expansion(n):
@@ -176,8 +178,8 @@
     to_occ_peers(lambda k, o: m_copy(k, o).start())
     vir[y, x, zl, half] = vir_ref[half]
 
+    each(1, NY, lambda k: y_copy(k).start())
     each(1, N_AO, lambda k: g_copy(k).wait())
-    each(1, NY, lambda k: y_copy(k).start())
     cols_f[...] = cols[...].astype(F32).reshape(N_AO * 16, 128)
     table = jnp.concatenate(
         [cols_f[pl.ds(d, 128, stride=8), :].astype(BF16) for d in range(8)], axis=1
@@ -249,15 +251,15 @@
             x_far[h][i].start()
 
     def z_copy(n):
-        ref = vir.at[n * 4:n * 4 + 4, :, zl, half]
-        return remote(ref, ref, z_s.at[n], z_r.at[n], (up, down)[n], ao_z)
+        ref = vir.at[(0, 5)[n]:(5, NY)[n], :, zl, half]
+        return remote(ref, ref, z_s.at[n], z_r.at[n], (outer, occ)[n], ao_z)
 
     def c_copy(n, lo, hi, zz):
         ref = vir.at[lo:hi, :, zz, half]
         return remote(ref, ref, c_s.at[n], c_r.at[n], sibling, ao)
 
     z_copies = [z_copy(0), z_copy(1)]
-    c_copies = [c_copy(0, 0, NY, zl), c_copy(1, 0, 4, 1 - zl), c_copy(2, 4, NY, 1 - zl)]
+    c_copies = [c_copy(0, 0, NY, zl), c_copy(1, 0, 5, 1 - zl), c_copy(2, 5, NY, 1 - zl)]
 
     def sort(n):
         for k in (0,) + OCC_ORDER:
@@ -327,42 +329,50 @@
     each(1, N_AO, end_first)
     each(0, N_AO, mark, unroll=2)
     collect(0)
+    order = jnp.where(
+        iota((128, 128), 1) == (iota((128, 128), 0) % 16) * 8 + iota((128, 128), 0) // 16, 1.0, 0.0
+    ).astype(BF16)
+
+    def chunk(n):
+        return pl.ds(pl.multiple_of(n * CHUNK, CHUNK), CHUNK)
+
+    def reorder(zz, lo, hi):
+        def columns(n):
+            for j in range(lo, hi):
+                got = dot(order, vir[j, :, zz, :, :, chunk(n)].reshape(128, CHUNK)).astype(BF16)
+                for si in range(8):
+                    virp[zz, si * 128 + j * 16:si * 128 + (j + 1) * 16, chunk(n)] = got[si * 16:(si + 1) * 16]
+
+        each(0, NVIR // CHUNK, columns)
+
+    c_copies[0].wait_recv()
+    reorder(zl, 0, NY)
     for n in range(2):
         z_copies[n].wait_recv()
         c_copies[n + 1].start()
     each(1, N_AO, lambda k: b_copy(1, k).wait())
     collect(1)
-    for copy in c_copies:
-        copy.wait_recv()
-
-    order = jnp.where(
-        iota((256, 256), 1) == (iota((256, 256), 0) % 32) * 8 + iota((256, 256), 0) // 32, 1.0, 0.0
-    ).astype(BF16)
-
-    def chunk(n):
-        return pl.ds(pl.multiple_of(n * CHUNK, CHUNK), CHUNK)
-
-    def reorder(n):
-        for j in range(NY):
-            got = dot(order, vir[j, :, :, :, :, chunk(n)].reshape(256, CHUNK)).astype(BF16)
-            for si in range(8):
-                virp[si * 256 + j * 32:si * 256 + (j + 1) * 32, chunk(n)] = got[si * 32:(si + 1) * 32]
-
-    each(0, NVIR // CHUNK, reorder)
-
-    for si in range(8):
-        for m in range(2):
-            hb[:, si * 256 + m * 128:si * 256 + (m + 1) * 128] = jnp.concatenate(
+    for m in range(2):
+        for si in range(8):
+            hb[m, :, si * 128:(si + 1) * 128] = jnp.concatenate(
                 [hf[2 * n + m, pl.ds(p * 64 + si, 8, stride=8), :] for p in range(P_LOC) for n in range(4)], axis=0
             ).astype(BF16)
 
     def v_copy(k, a=0):
         return remote(vs.at[a], vd.at[ao], v_s.at[k], v_r.at[k], occ, a)
 
+    def first_own(n):
+        acc[:, chunk(n)] = dot(hb[zl], virp[zl, :, chunk(n)])
+
     def first(n):
-        rows_v = dot(hb[...], virp[:, chunk(n)]).astype(BF16).astype(F32)
-        vt[chunk(n)] = rows_v.T
-
+        rows_v = acc[:, chunk(n)] + dot(hb[1 - zl], virp[1 - zl, :, chunk(n)])
+        vt[chunk(n)] = rows_v.astype(BF16).astype(F32).T
+
+    each(0, NVIR // CHUNK, first_own)
+    c_copies[1].wait_recv()
+    reorder(1 - zl, 0, 5)
+    c_copies[2].wait_recv()
+    reorder(1 - zl, 5, NY)
     each(0, NVIR // CHUNK, first)
     vt[NVIR:] = jnp.zeros((8, 128), F32)
     for s in range(N_AO):
@@ -412,7 +422,7 @@
             vmem((N_AO, 16, 128), BF16),
             vmem((N_AO * 16, 128), F32),
             vmem((NY, NX, NZ, 2, 16, NVIR), BF16),
-            vmem((N_AO * 32, NVIR), BF16),
+            vmem((2, N_AO * 16, NVIR), BF16),
             vmem((32 * TILES, 128), F32),
             vmem((TILES, 128, 128), BF16),
             vmem((2, 16, 256, 128), BF16),
@@ -429,7 +439,7 @@
             vmem((N_AO, 1, 128), F32),
             vmem((N_AO, SLOTS, 1024), BF16),
             vmem((8, 256, 128), F32),
-            vmem((128, 2048), BF16),
+            vmem((2, 128, 1024), BF16),
             vmem((NVIR + 8, 128), F32),
             vmem((N_AO, B_PAD, 128), BF16),
             vmem((N_AO, B_PAD, 128), BF16),

time: 122 us -> 118 us (0.967); the launches traced: 121 us -> 118 us
  Pallas kernels: 117 us -> 114 us
    pallas_call x1, Pallas kernels: 117 us -> 114 us  [shards(): pl.pallas_call(kernel, out_shape=jax.ShapeDtypeStruct((P_LOC, B_LOC, NVIR...]
where the time goes in v4:
time: 118 us
  Pallas kernels  114 us (97%)
  local copies, waits for them, and re-layouts  3.94 us (3%)
    pallas_call x1, Pallas kernels, shards(): pl.pallas_call(kernel, out_shape=jax.ShapeDtypeStruct((P_LOC, B_LOC, NVIR...  114 us
    pallas_call x1, local copies, waits for them, and re-layouts, shards(): pl.pallas_call(kernel, out_shape=jax.ShapeDtypeStruct((P_LOC, B_LOC, NVIR...  2.58 us

profile of v4, /device:TPU:56, one launch (start us, length us, event | category | flops | bytes accessed | tf_op | source)
XLA Modules:
  0.0 118.2 jit_solution(12877591153416396911)
XLA Ops:
  0.0 0.8 tile.10
  0.8 0.6 tile.12.pairs_ref
  1.4 114.2 %shard_map.73 = f32[4,28,1792]{2,1,0:T(8,128)} custom-call(bf16[192,4096]{1,0:T(8,128)(2,1)} %ints_ref.1, s32[1,192]{1,0:T(1,128)} %bitcast.7, s32[3,192]{1,0:T(4,128)} %bitcast.6, s32[1,192]{1,0:T(1,128)} %bitcast.8, s32[1,128]{1,0:T(1,128)} %tile.12.pairs_ref, bf16[32,256]{1,0:T(8,128)(2,1)} %occ_ref.1, bf16[2,16,1792]{2,1,0:T(8,128)(2,1)} %bitcast.5), custom_call_target="tpu_custom_call" | custom-call | tf_op jit(solution)/shard_map/pallas_call | solution.py:416
  115.6 2.6 %copy.8 = f32[4,28,1792]{2,0,1:T(4,128)} copy(f32[4,28,1792]{2,1,0:T(8,128)} %shard_map.73) | data formatting | bytes 1605632 | tf_op jit(solution)/shard_map/pallas_call | solution.py:416
  (1 shorter events, 0.0 us)

commit v5 on v4

--- a/solution.py
+++ b/solution.py
@@ -327,7 +327,7 @@
             hf[2 * m + 1, n * 128:(n + 1) * 128] = total[:, 128:]
 
     each(1, N_AO, end_first)
-    each(0, N_AO, mark, unroll=2)
+    each(0, N_AO, mark, unroll=4)
     collect(0)
     order = jnp.where(
         iota((128, 128), 1) == (iota((128, 128), 0) % 16) * 8 + iota((128, 128), 0) // 16, 1.0, 0.0
@@ -350,6 +350,10 @@
     for n in range(2):
         z_copies[n].wait_recv()
         c_copies[n + 1].start()
+    c_copies[1].wait_recv()
+    reorder(1 - zl, 0, 5)
+    c_copies[2].wait_recv()
+    reorder(1 - zl, 5, NY)
     each(1, N_AO, lambda k: b_copy(1, k).wait())
     collect(1)
     for m in range(2):
@@ -369,10 +373,6 @@
         vt[chunk(n)] = rows_v.astype(BF16).astype(F32).T
 
     each(0, NVIR // CHUNK, first_own)
-    c_copies[1].wait_recv()
-    reorder(1 - zl, 0, 5)
-    c_copies[2].wait_recv()
-    reorder(1 - zl, 5, NY)
     each(0, NVIR // CHUNK, first)
     vt[NVIR:] = jnp.zeros((8, 128), F32)
     for s in range(N_AO):

time: 118 us -> 122 us (1.034); the launches traced: 118 us -> 121 us
  Pallas kernels: 114 us -> 117 us
    pallas_call x1, Pallas kernels: 114 us -> 117 us  [shards(): pl.pallas_call(kernel, out_shape=jax.ShapeDtypeStruct((P_LOC, B_LOC, NVIR...]
where the time goes in v5:
time: 122 us; the launch traced here: 121 us
  Pallas kernels  117 us (96%)
  local copies, waits for them, and re-layouts  3.94 us (3%)
    pallas_call x1, Pallas kernels, shards(): pl.pallas_call(kernel, out_shape=jax.ShapeDtypeStruct((P_LOC, B_LOC, NVIR...  117 us
    pallas_call x1, local copies, waits for them, and re-layouts, shards(): pl.pallas_call(kernel, out_shape=jax.ShapeDtypeStruct((P_LOC, B_LOC, NVIR...  2.58 us

profile of v5, /device:TPU:56, one launch (start us, length us, event | category | flops | bytes accessed | tf_op | source)
XLA Modules:
  0.0 120.8 jit_solution(4046369342408455308)
XLA Ops:
  0.0 0.8 tile.10
  0.8 0.6 tile.12.pairs_ref
  1.4 116.9 %shard_map.73 = f32[4,28,1792]{2,1,0:T(8,128)} custom-call(bf16[192,4096]{1,0:T(8,128)(2,1)} %ints_ref.1, s32[1,192]{1,0:T(1,128)} %bitcast.7, s32[3,192]{1,0:T(4,128)} %bitcast.6, s32[1,192]{1,0:T(1,128)} %bitcast.8, s32[1,128]{1,0:T(1,128)} %tile.12.pairs_ref, bf16[32,256]{1,0:T(8,128)(2,1)} %occ_ref.1, bf16[2,16,1792]{2,1,0:T(8,128)(2,1)} %bitcast.5), custom_call_target="tpu_custom_call" | custom-call | tf_op jit(solution)/shard_map/pallas_call | solution.py:416
  118.3 2.6 %copy.8 = f32[4,28,1792]{2,0,1:T(4,128)} copy(f32[4,28,1792]{2,1,0:T(8,128)} %shard_map.73) | data formatting | bytes 1605632 | tf_op jit(solution)/shard_map/pallas_call | solution.py:416
  (1 shorter events, 0.0 us)
